TPU v7x, 512 devices: a whole 4x4x16 slice. The times are simulated.
512 devices in a mesh: avg: 16 (over x, y_lo, core), space: 32 (over z, y_hi).
Axes of the slice: x: 4, y: 4 (y_hi: 2, y_lo: 2; y = y_hi * 2 + y_lo), z: 16, core: 2. Of those that a mesh axis runs over, the one named last changes fastest.
Arguments:
- spectral_state: float32 [3, 2, 1024, 1024], P(None, None, 'space', 'avg'), may hold values from -6 to 6
- phase_index: int32 [16], P('avg'), may hold values from 0 to 63
- weight_count: int32 [16], P('avg'), may hold values from 1 to 7
Outputs:
- advanced: float32 [3, 2, 1024, 1024], P(None, None, 'space', 'avg')
All inputs are finite; a program needn't handle non-finite values.
Results may differ from a plain program's by a relative error of at most 0.015.
Values may be sent and summed in bfloat16 or wider, within the bound.
No kernel may reach another device: no remote copies, remote signals or barrier semaphores. Data moves between devices by JAX's collectives and lax.ppermute only.
A program may use at most 64 MiB of HBM per device.

v0:
```python
import math

import jax
import jax.numpy as jnp
import numpy as np
from jax import lax
from jax.experimental import pallas as pl
from jax.experimental.pallas import tpu as pltpu
from jax.sharding import PartitionSpec as P

N = 1024
LANES = 128
ROWS = 32
HALF = 16

coriolis = 1.0
wave_speed = 6.0
phase_step = 0.25
time_step = 2.0
weight_scale = 64.0

VMEM_LIMIT = 28 * 1024 * 1024
F32 = jnp.float32
BF16 = jnp.bfloat16


def fourier_tables():
    positions = np.arange(N, dtype=np.int64)
    angles = (positions[:, None] * positions[None, :] % N).astype(np.float64) * (2.0 * math.pi / N)
    return jnp.asarray(np.cos(angles), BF16), jnp.asarray(np.sin(angles), BF16)


def wave_of(index):
    shifted = jnp.where(index >= N // 2, index - N, index)
    return shifted.astype(F32) * (2.0 / N)


def sine_cosine(angle):
    turns = jnp.floor(angle * (2.0 / math.pi) + 0.5)
    rest = angle - turns * 1.5703125
    rest = rest - turns * 4.837512969970703125e-4
    rest = rest - turns * 7.54978995489188216e-8
    square = rest * rest
    sine = ((-1.9515295891e-4 * square + 8.3321608736e-3) * square - 1.6666654611e-1) * square * rest + rest
    cosine = ((2.443315711809948e-5 * square - 1.388731625493765e-3) * square + 4.166664568298827e-2) * square * square
    cosine = cosine - 0.5 * square + 1.0
    quarter = turns.astype(jnp.int32)
    odd = (quarter & 1) == 1
    sine_out = jnp.where(odd, cosine, sine)
    cosine_out = jnp.where(odd, sine, cosine)
    sine_out = jnp.where((quarter & 2) == 2, -sine_out, sine_out)
    cosine_out = jnp.where(((quarter + 1) & 2) == 2, -cosine_out, cosine_out)
    return sine_out, cosine_out


def exponential_terms(wave_rows, wave_columns, phase_value):
    squared = coriolis * coriolis + (wave_speed * wave_speed) * (
        wave_rows * wave_rows + wave_columns * wave_columns
    )
    inverse = lax.rsqrt(squared)
    inverse = inverse * (1.5 - 0.5 * squared * inverse * inverse)
    sine, cosine = sine_cosine(squared * inverse * phase_value)
    return sine * inverse, (1.0 - cosine) * (inverse * inverse)


def wave_operator(fields, speed_rows, speed_columns):
    east_r, east_i, north_r, north_i, height_r, height_i = fields
    return (
        coriolis * north_r + speed_rows * height_i,
        coriolis * north_i - speed_rows * height_r,
        speed_columns * height_i - coriolis * east_r,
        -speed_columns * height_r - coriolis * east_i,
        speed_rows * east_i + speed_columns * north_i,
        -(speed_rows * east_r + speed_columns * north_r),
    )


def wave_exponential(fields, wave_rows, wave_columns, sine_term, cosine_term):
    speed_rows = wave_speed * wave_rows
    speed_columns = wave_speed * wave_columns
    single = wave_operator(fields, speed_rows, speed_columns)
    double = wave_operator(single, speed_rows, speed_columns)
    return [w + sine_term * a + cosine_term * b for w, a, b in zip(fields, single, double)]


def lanes_of(rows):
    return lax.broadcasted_iota(jnp.int32, (rows, LANES), 1)


def swap_halves(even, odd):
    low = lanes_of(even.shape[0]) < 64
    return (
        jnp.where(low, even, pltpu.roll(odd, 64, 1)),
        jnp.where(low, pltpu.roll(even, 64, 1), odd),
    )


def swap_quarters(parts):
    lane = lanes_of(parts[0].shape[0])
    odd = (lane & 32) == 32
    first, second, third, fourth = parts
    first, second = (
        jnp.where(odd, pltpu.roll(second, 32, 1), first),
        jnp.where(odd, second, pltpu.roll(first, 96, 1)),
    )
    third, fourth = (
        jnp.where(odd, pltpu.roll(fourth, 32, 1), third),
        jnp.where(odd, fourth, pltpu.roll(third, 96, 1)),
    )
    first, third = swap_halves(first, third)
    second, fourth = swap_halves(second, fourth)
    return first, second, third, fourth


def spread_kernel(state_ref, out_ref):
    for plane in range(6):
        low = state_ref[plane // 2, plane % 2, :HALF, :]
        high = state_ref[plane // 2, plane % 2, HALF:, :]
        packed = jnp.concatenate([low, high], axis=1).astype(BF16)
        for target in range(16):
            out_ref[target, HALF * plane : HALF * (plane + 1), :] = packed


def first_kernel(phase_ref, gathered_ref, cosine_ref, sine_ref, out_ref, rotated):
    phase_value = phase_ref[0].astype(F32) * phase_step
    row_start = lax.axis_index("space") * ROWS
    for group in range(8):
        planes = []
        for plane in range(6):
            rows = slice(HALF * plane, HALF * (plane + 1))
            planes.append(
                swap_halves(
                    gathered_ref[2 * group, rows, :].astype(F32),
                    gathered_ref[2 * group + 1, rows, :].astype(F32),
                )
            )
        wave_columns = wave_of(lanes_of(HALF) + LANES * group)
        for half in range(2):
            row = lax.broadcasted_iota(jnp.int32, (HALF, LANES), 0) + (row_start + HALF * half)
            wave_rows = wave_of(row)
            terms = exponential_terms(wave_rows, wave_columns, phase_value)
            result = wave_exponential([p[half] for p in planes], wave_rows, wave_columns, *terms)
            for plane in range(6):
                start = ROWS * plane + HALF * half
                rotated[start : start + HALF, LANES * group : LANES * (group + 1)] = result[
                    plane
                ].astype(BF16)
    for chunk in range(4):
        columns = slice(256 * chunk, 256 * (chunk + 1))
        data = rotated[...]
        cosine = jnp.dot(data, cosine_ref[:, columns], preferred_element_type=F32)
        sine = jnp.dot(data, sine_ref[:, columns], preferred_element_type=F32)
        for part in range(2):
            lanes = slice(LANES * part, LANES * (part + 1))
            real, imag = [], []
            for field in range(3):
                top = slice(64 * field, 64 * field + ROWS)
                bottom = slice(64 * field + ROWS, 64 * (field + 1))
                real.append(cosine[top, lanes] - sine[bottom, lanes])
                imag.append(sine[top, lanes] + cosine[bottom, lanes])
            main = swap_quarters([real[0], real[1], real[2], imag[0]])
            extra = swap_quarters(
                [imag[1][:HALF], imag[2][:HALF], imag[1][HALF:], imag[2][HALF:]]
            )
            for offset in range(4):
                target = 8 * chunk + 4 * part + offset
                out_ref[target, :ROWS, :] = main[offset].astype(BF16)
                out_ref[target, ROWS:, :] = extra[offset].astype(BF16)


def second_kernel(arrived_ref, cosine_ref, sine_ref, out_ref, real_part, imag_part, pairs):
    lane = lanes_of(HALF)
    first = lane < 32
    for source in range(32):
        for half in range(2):
            rows = slice(HALF * half, HALF * (half + 1))
            main = arrived_ref[source, rows, :]
            target = slice(ROWS * source + HALF * half, ROWS * source + HALF * (half + 1))
            real_part[target, :] = main
            rest = arrived_ref[source, ROWS:, :].astype(F32)
            rest = pltpu.roll(rest, 96 if half else 32, 1)
            imag = jnp.where(first, pltpu.roll(main.astype(F32), 32, 1), rest)
            imag_part[target, :] = (-imag).astype(BF16)
    lane = lanes_of(256)
    quarter = lane // 32
    for chunk in range(4):
        rows = slice(256 * chunk, 256 * (chunk + 1))
        grid = jnp.dot(cosine_ref[rows, :], real_part[...], preferred_element_type=F32)
        grid = grid + jnp.dot(sine_ref[rows, :], imag_part[...], preferred_element_type=F32)
        grid = grid * (1.0 / N)
        up = pltpu.roll(grid, 32, 1)
        down = pltpu.roll(grid, 96, 1)
        left = jnp.where(quarter == 0, grid, jnp.where(quarter == 3, down, up))
        right = jnp.where(quarter < 2, grid, up)
        pairs[rows, :LANES] = (left * right).astype(BF16)
        pairs[rows, LANES:] = (grid * down).astype(BF16)
    lane = lanes_of(HALF)
    quarter = lane // 32
    for chunk in range(4):
        rows = slice(256 * chunk, 256 * (chunk + 1))
        real = jnp.dot(cosine_ref[rows, :], pairs[...], preferred_element_type=F32)
        imag = -jnp.dot(sine_ref[rows, :], pairs[...], preferred_element_type=F32)
        for offset in range(8):
            target = 8 * chunk + offset
            top = slice(ROWS * offset, ROWS * offset + HALF)
            bottom = slice(ROWS * offset + HALF, ROWS * (offset + 1))
            both = slice(ROWS * offset, ROWS * (offset + 1))
            out_ref[target, :ROWS, :] = real[both, :LANES].astype(BF16)
            out_ref[target, ROWS : 2 * ROWS, :] = imag[both, :LANES].astype(BF16)
            extra = jnp.where(
                quarter < 2,
                jnp.where(quarter == 0, pltpu.roll(real[top, LANES:], 96, 1), real[bottom, LANES:]),
                jnp.where(
                    quarter == 2,
                    pltpu.roll(imag[top, LANES:], 32, 1),
                    pltpu.roll(imag[bottom, LANES:], 64, 1),
                ),
            )
            out_ref[target, 2 * ROWS :, :] = extra.astype(BF16)


def third_kernel(phase_ref, weight_ref, returned_ref, cosine_ref, sine_ref, out_ref, lines):
    phase_value = phase_ref[0].astype(F32) * phase_step
    weight = weight_ref[0].astype(F32) * (1.0 / weight_scale)
    row_start = lax.axis_index("space") * ROWS
    for group in range(8):
        columns = slice(LANES * group, LANES * (group + 1))
        for part in range(2):
            rows = slice(ROWS * part, ROWS * (part + 1))
            blocks = swap_quarters(
                [returned_ref[4 * group + offset, rows, :].astype(F32) for offset in range(4)]
            )
            for product in range(4):
                start = 160 * part + ROWS * product
                lines[start : start + ROWS, columns] = blocks[product].astype(BF16)
        blocks = swap_quarters(
            [returned_ref[4 * group + offset, 2 * ROWS :, :].astype(F32) for offset in range(4)]
        )
        for index in range(4):
            start = 160 * (index // 2) + 128 + HALF * (index % 2)
            lines[start : start + HALF, columns] = blocks[index].astype(BF16)
    for chunk in range(4):
        columns = slice(256 * chunk, 256 * (chunk + 1))
        data = lines[...]
        cosine = jnp.dot(data, cosine_ref[:, columns], preferred_element_type=F32)
        sine = jnp.dot(data, sine_ref[:, columns], preferred_element_type=F32)
        for part in range(2):
            lanes = slice(LANES * part, LANES * (part + 1))
            group = 2 * chunk + part
            wave_columns = wave_of(lanes_of(HALF) + LANES * group)
            halves = []
            for half in range(2):
                row = lax.broadcasted_iota(jnp.int32, (HALF, LANES), 0) + (row_start + HALF * half)
                wave_rows = wave_of(row)
                real, imag = [], []
                for product in range(5):
                    start = ROWS * product + HALF * half
                    top = slice(start, start + HALF)
                    bottom = slice(160 + start, 160 + start + HALF)
                    real.append((cosine[top, lanes] + sine[bottom, lanes]) * (1.0 / N))
                    imag.append((cosine[bottom, lanes] - sine[top, lanes]) * (1.0 / N))
                tendency = []
                for toward_east, toward_north in ((0, 1), (1, 2), (3, 4)):
                    tendency.append(wave_rows * imag[toward_east] + wave_columns * imag[toward_north])
                    tendency.append(
                        -(wave_rows * real[toward_east] + wave_columns * real[toward_north])
                    )
                sine_term, cosine_term = exponential_terms(wave_rows, wave_columns, phase_value)
                result = wave_exponential(
                    tendency, wave_rows, wave_columns, -sine_term, cosine_term
                )
                halves.append([weight * plane for plane in result])
            for plane in range(6):
                even, odd = swap_halves(halves[0][plane], halves[1][plane])
                rows = slice(HALF * plane, HALF * (plane + 1))
                out_ref[2 * group, rows, :] = even.astype(BF16)
                out_ref[2 * group + 1, rows, :] = odd.astype(BF16)


def last_kernel(state_ref, parts_ref, out_ref):
    lane = lanes_of(HALF)
    high = lane >= 64
    column = (lane & 63) + lax.axis_index("avg") * 64
    row = lax.broadcasted_iota(jnp.int32, (HALF, LANES), 0) + lax.axis_index("space") * ROWS
    wave_rows = wave_of(jnp.where(high, row + HALF, row))
    wave_columns = wave_of(column)
    fields = []
    for plane in range(6):
        rows = slice(HALF * plane, HALF * (plane + 1))
        total = parts_ref[0, rows, :].astype(F32)
        for source in range(1, 16):
            total = total + parts_ref[source, rows, :].astype(F32)
        low_rows = state_ref[plane // 2, plane % 2, :HALF, :]
        high_rows = state_ref[plane // 2, plane % 2, HALF:, :]
        fields.append(jnp.concatenate([low_rows, high_rows], axis=1) + time_step * total)
    terms = exponential_terms(wave_rows, wave_columns, time_step)
    result = wave_exponential(fields, wave_rows, wave_columns, *terms)
    for plane in range(6):
        out_ref[plane // 2, plane % 2, :HALF, :] = result[plane][:, :64]
        out_ref[plane // 2, plane % 2, HALF:, :] = result[plane][:, 64:]


def call(kernel, name, shape, dtype, scratch, places):
    spots = [pl.BlockSpec(memory_space=pltpu.SMEM if p == "s" else pltpu.VMEM) for p in places]
    return pl.pallas_call(
        kernel,
        name=name,
        out_shape=jax.ShapeDtypeStruct(shape, dtype),
        in_specs=spots,
        out_specs=pl.BlockSpec(memory_space=pltpu.VMEM),
        scratch_shapes=[pltpu.VMEM(s, BF16) for s in scratch],
        compiler_params=pltpu.CompilerParams(vmem_limit_bytes=VMEM_LIMIT),
    )


def per_device(spectral_state, phase_index, weight_count):
    cosine_table, sine_table = fourier_tables()
    spread = call(spread_kernel, "spread", (16, 96, LANES), BF16, [], "v")(spectral_state)
    gathered = lax.all_to_all(spread, "avg", 0, 0)
    outgoing = call(first_kernel, "inverse_columns", (32, 48, LANES), BF16, [(192, N)], "svvv")(
        phase_index, gathered, cosine_table, sine_table
    )
    arrived = lax.all_to_all(outgoing, "space", 0, 0)
    outgoing_back = call(
        second_kernel,
        "grid_products",
        (32, 80, LANES),
        BF16,
        [(N, LANES), (N, LANES), (N, 2 * LANES)],
        "vvv",
    )(arrived, cosine_table, sine_table)
    returned = lax.all_to_all(outgoing_back, "space", 0, 0)
    weighted = call(third_kernel, "forward_columns", (16, 96, LANES), BF16, [(320, N)], "ssvvv")(
        phase_index, weight_count, returned, cosine_table, sine_table
    )
    parts = lax.all_to_all(weighted, "avg", 0, 0)
    return call(last_kernel, "advance", spectral_state.shape, F32, [], "vv")(spectral_state, parts)


def solution(mesh):
    in_specs = (P(None, None, "space", "avg"), P("avg"), P("avg"))
    out_specs = P(None, None, "space", "avg")
    return jax.shard_map(
        per_device, mesh=mesh, in_specs=in_specs, out_specs=out_specs, check_vma=False
    )
```

profile of v0, /device:TPU:24, one launch (start us, length us, event | category | flops | bytes accessed | tf_op | source)
XLA Modules:
  0.0 129.2 jit_solution(6270528348608299232)
XLA Ops:
  0.0 0.0 copy-start.5
  0.0 0.9 copy-done.5
  0.9 0.8 spread.1
  1.7 5.8 %all-to-all-start = ((bf16[16,96,128]{2,1,0:T(8,128)(2,1)}), bf16[16,96,128]{2,1,0:T(8,128)(2,1)S(1)}, u32[]{:S(2)}, u32[]{:S(2)}) async-start(bf16[16,96,128]{2,1,0:T(8,128)(2,1)} %spread.1), calls=%async_computation | async-start | bytes 786432 | tf_op jit(solution)/shard_map/all_to_all | solution.py:319
  8.2 7.3 %all-to-all-done.gathered_ref = bf16[16,96,128]{2,1,0:T(8,128)(2,1)S(1)} async-done(((bf16[16,96,128]{2,1,0:T(8,128)(2,1)}), bf16[16,96,128]{2,1,0:T(8,128)(2,1)S(1)}, u32[]{:S(2)}, u32[]{:S(2)}) %all-to-all-start) | async-done | bytes 393248 | tf_op jit(solution)/shard_map/all_to_all | solution.py:319
  15.4 0.0 copy-start
  15.4 1.6 %copy-done = bf16[1024,1024]{1,0:T(8,128)(2,1)S(1)} copy-done((bf16[1024,1024]{1,0:T(8,128)(2,1)S(1)}, bf16[1024,1024]{1,0:T(8,128)(2,1)}, u32[]{:S(2)}) %copy-start) | copy-done | bytes 2097176
  17.0 0.0 copy-start.2
  17.0 1.6 %copy-done.2 = bf16[1024,1024]{1,0:T(8,128)(2,1)S(1)} copy-done((bf16[1024,1024]{1,0:T(8,128)(2,1)S(1)}, bf16[1024,1024]{1,0:T(8,128)(2,1)}, u32[]{:S(2)}) %copy-start.2) | copy-done | bytes 2097176
  18.6 0.0 copy-start.1
  18.6 0.0 copy-start.3
  18.6 1.7 %inverse_columns.1 = bf16[32,48,128]{2,1,0:T(8,128)(2,1)S(1)} custom-call(s32[1]{0:T(128)S(6)} %copy.6.phase_ref, bf16[16,96,128]{2,1,0:T(8,128)(2,1)S(1)} %all-to-all-done.gathered_ref, bf16[1024,1024]{1,0:T(8,128)(2,1)S(1)} %copy-done, bf16[1024,1024]{1,0:T(8,128)(2,1)S(1)} %copy-done.2), custom_call_target="tpu_custom_call" | custom-call | tf_op jit(solution)/shard_map/inverse_columns/pallas_call | solution.py:320
  20.4 45.6 %all_to_all.20.arrived_ref = bf16[32,48,128]{2,1,0:T(8,128)(2,1)S(1)} all-to-all(bf16[32,48,128]{2,1,0:T(8,128)(2,1)S(1)} %inverse_columns.1), channel_id=1, replica_groups=mesh['avg'=16,'space'=32] {'space'}, dimensions={0} | all-to-all | bytes 786432 | tf_op jit(solution)/shard_map/all_to_all | solution.py:323
  66.0 0.0 copy-done.1
  66.0 0.0 copy-done.3
  66.0 3.4 %grid_products.1 = bf16[32,80,128]{2,1,0:T(8,128)(2,1)} custom-call(bf16[32,48,128]{2,1,0:T(8,128)(2,1)S(1)} %all_to_all.20.arrived_ref, bf16[1024,1024]{1,0:T(8,128)(2,1)S(1)} %copy-done.1, bf16[1024,1024]{1,0:T(8,128)(2,1)S(1)} %copy-done.3), custom_call_target="tpu_custom_call" | custom-call | tf_op jit(solution)/shard_map/grid_products/pallas_call | solution.py:324
  69.4 5.1 %all-to-all-start.2 = ((bf16[32,80,128]{2,1,0:T(8,128)(2,1)}), bf16[32,80,128]{2,1,0:T(8,128)(2,1)S(1)}, u32[]{:S(2)}, u32[]{:S(2)}) async-start(bf16[32,80,128]{2,1,0:T(8,128)(2,1)} %grid_products.1), calls=%async_computation.2 | async-start | bytes 1310720 | tf_op jit(solution)/shard_map/all_to_all | solution.py:332
  75.2 37.5 %all-to-all-done.2.returned_ref = bf16[32,80,128]{2,1,0:T(8,128)(2,1)S(1)} async-done(((bf16[32,80,128]{2,1,0:T(8,128)(2,1)}), bf16[32,80,128]{2,1,0:T(8,128)(2,1)S(1)}, u32[]{:S(2)}, u32[]{:S(2)}) %all-to-all-start.2) | async-done | bytes 655392 | tf_op jit(solution)/shard_map/all_to_all | solution.py:332
  112.7 0.0 copy-start.4
  112.7 1.6 %copy-done.4 = bf16[1024,1024]{1,0:T(8,128)(2,1)S(1)} copy-done((bf16[1024,1024]{1,0:T(8,128)(2,1)S(1)}, bf16[1024,1024]{1,0:T(8,128)(2,1)}, u32[]{:S(2)}) %copy-start.4) | copy-done | bytes 2097176
  114.3 2.6 %forward_columns.1 = bf16[16,96,128]{2,1,0:T(8,128)(2,1)S(1)} custom-call(s32[1]{0:T(128)S(6)} %copy.6.phase_ref, s32[1]{0:T(128)S(6)} %copy.7.weight_ref, bf16[32,80,128]{2,1,0:T(8,128)(2,1)S(1)} %all-to-all-done.2.returned_ref, bf16[1024,1024]{1,0:T(8,128)(2,1)S(1)} %copy-done.1, bf16[1024,1024]{1,0:T(8,128)(2,1)S(1)} %copy-done.4), custom_call_target="tpu_custom_call" | custom-call | tf_op jit(solution)/shard_map/forward_columns/pallas_call | solution.py:333
  116.9 11.5 %all_to_all.21.parts_ref = bf16[16,96,128]{2,1,0:T(8,128)(2,1)S(1)} all-to-all(bf16[16,96,128]{2,1,0:T(8,128)(2,1)S(1)} %forward_columns.1), channel_id=1, replica_groups=mesh['avg'=16,'space'=32] {'avg'}, dimensions={0} | all-to-all | bytes 786432 | tf_op jit(solution)/shard_map/all_to_all | solution.py:336
  128.4 0.0 copy-done.6
  128.4 0.8 advance.1
  (1 shorter events, 0.0 us)
Async XLA Ops:
  0.0 0.9 copy-start.5
  1.7 13.7 %all-to-all-start = ((bf16[16,96,128]{2,1,0:T(8,128)(2,1)}), bf16[16,96,128]{2,1,0:T(8,128)(2,1)S(1)}, u32[]{:S(2)}, u32[]{:S(2)}) async-start(bf16[16,96,128]{2,1,0:T(8,128)(2,1)} %spread.1), calls=%async_computation | async-start | bytes 786432 | tf_op jit(solution)/shard_map/all_to_all | solution.py:319
  15.4 1.6 %copy-start = (bf16[1024,1024]{1,0:T(8,128)(2,1)S(1)}, bf16[1024,1024]{1,0:T(8,128)(2,1)}, u32[]{:S(2)}) copy-start(bf16[1024,1024]{1,0:T(8,128)(2,1)} %constant.4.clone.cosine_ref) | copy-start | bytes 6291460
  17.0 1.6 %copy-start.2 = (bf16[1024,1024]{1,0:T(8,128)(2,1)S(1)}, bf16[1024,1024]{1,0:T(8,128)(2,1)}, u32[]{:S(2)}) copy-start(bf16[1024,1024]{1,0:T(8,128)(2,1)} %constant.5.clone.sine_ref) | copy-start | bytes 6291460
  18.6 47.4 %copy-start.1 = (bf16[1024,1024]{1,0:T(8,128)(2,1)S(1)}, bf16[1024,1024]{1,0:T(8,128)(2,1)}, u32[]{:S(2)}) copy-start(bf16[1024,1024]{1,0:T(8,128)(2,1)} %constant.4.clone.cosine_ref) | copy-start | bytes 6291460
  18.6 47.4 %copy-start.3 = (bf16[1024,1024]{1,0:T(8,128)(2,1)S(1)}, bf16[1024,1024]{1,0:T(8,128)(2,1)}, u32[]{:S(2)}) copy-start(bf16[1024,1024]{1,0:T(8,128)(2,1)} %constant.5.clone.sine_ref) | copy-start | bytes 6291460
  69.4 43.3 %all-to-all-start.2 = ((bf16[32,80,128]{2,1,0:T(8,128)(2,1)}), bf16[32,80,128]{2,1,0:T(8,128)(2,1)S(1)}, u32[]{:S(2)}, u32[]{:S(2)}) async-start(bf16[32,80,128]{2,1,0:T(8,128)(2,1)} %grid_products.1), calls=%async_computation.2 | async-start | bytes 1310720 | tf_op jit(solution)/shard_map/all_to_all | solution.py:332
  112.7 1.6 %copy-start.4 = (bf16[1024,1024]{1,0:T(8,128)(2,1)S(1)}, bf16[1024,1024]{1,0:T(8,128)(2,1)}, u32[]{:S(2)}) copy-start(bf16[1024,1024]{1,0:T(8,128)(2,1)} %constant.5.clone.sine_ref) | copy-start | bytes 6291460
  114.3 14.1 %copy-start.6 = (f32[3,2,32,64]{3,2,1,0:T(8,128)S(1)}, f32[3,2,32,64]{3,2,1,0:T(8,128)}, u32[]{:S(2)}) copy-start(f32[3,2,32,64]{3,2,1,0:T(8,128)} %state_ref.3) | copy-start | bytes 147460
where the time goes:
time: 131 us; the launch traced here: 129 us
  blocking collectives  57.1 us (44%)
  waiting for transfers between devices  44.7 us (34%)
  starting transfers between devices  10.9 us (8%)
  Pallas kernels  9.45 us (7%)
  local copies, waits for them, and re-layouts  5.68 us (4%)
  between operations  1.33 us (1%)
    all_to_all x1, blocking collectives, per_device(): arrived = lax.all_to_all(outgoing, 'space', 0, 0)  45.6 us
    all_to_all x1, waiting for transfers between devices, per_device(): returned = lax.all_to_all(outgoing_back, 'space', 0, 0)  37.5 us
    all_to_all x1, blocking collectives, per_device(): parts = lax.all_to_all(weighted, 'avg', 0, 0)  11.5 us
    all_to_all x1, waiting for transfers between devices, per_device(): gathered = lax.all_to_all(spread, 'avg', 0, 0)  7.25 us
    all_to_all x1, starting transfers between devices, per_device(): gathered = lax.all_to_all(spread, 'avg', 0, 0)  5.77 us
    unnamed x14, local copies, waits for them, and re-layouts  5.68 us
    all_to_all x1, starting transfers between devices, per_device(): returned = lax.all_to_all(outgoing_back, 'space', 0, 0)  5.15 us
    pallas_call x1, Pallas kernels, per_device(): call(second_kernel, 'grid_products', (32, 80, LANES), BF16, [(N, LANES),...  3.43 us
  transfers between devices with their start and end apart: 2, of which 2 were waited for; matrix products, arithmetic and copies ran while one was open for 0% of the time, Pallas kernels for 0%

commit v1 on v0

v1 whole, which is shorter than its diff:
```python
import math

import jax
import jax.numpy as jnp
import numpy as np
from jax import lax
from jax.experimental import pallas as pl
from jax.experimental.pallas import tpu as pltpu
from jax.sharding import Mesh
from jax.sharding import PartitionSpec as P

N = 1024
LANES = 128
ROWS = 32
LINES = 16

coriolis = 1.0
wave_speed = 6.0
phase_step = 0.25
time_step = 2.0
weight_scale = 64.0

VMEM_LIMIT = 28 * 1024 * 1024
F32 = jnp.float32
BF16 = jnp.bfloat16
MAIN_AXES = ("zb", "zm", "yh")
GROUP_AXES = ("xy", "c", "zm", "yh")


def fourier_tables():
    positions = np.arange(N, dtype=np.int64)
    angles = (positions[:, None] * positions[None, :] % N).astype(np.float64) * (2.0 * math.pi / N)
    return jnp.asarray(np.stack([np.cos(angles), np.sin(angles)]), BF16)


def wave_of(index):
    shifted = jnp.where(index >= N // 2, index - N, index)
    return shifted.astype(F32) * (2.0 / N)


def sine_cosine(angle):
    turns = jnp.floor(angle * (2.0 / math.pi) + 0.5)
    rest = angle - turns * 1.5703125
    rest = rest - turns * 4.837512969970703125e-4
    rest = rest - turns * 7.54978995489188216e-8
    square = rest * rest
    sine = ((-1.9515295891e-4 * square + 8.3321608736e-3) * square - 1.6666654611e-1) * square * rest + rest
    cosine = ((2.443315711809948e-5 * square - 1.388731625493765e-3) * square + 4.166664568298827e-2) * square * square
    cosine = cosine - 0.5 * square + 1.0
    quarter = turns.astype(jnp.int32)
    odd = (quarter & 1) == 1
    sine_out = jnp.where(odd, cosine, sine)
    cosine_out = jnp.where(odd, sine, cosine)
    sine_out = jnp.where((quarter & 2) == 2, -sine_out, sine_out)
    cosine_out = jnp.where(((quarter + 1) & 2) == 2, -cosine_out, cosine_out)
    return sine_out, cosine_out


def exponential_terms(wave_rows, wave_columns, phase_value):
    squared = coriolis * coriolis + (wave_speed * wave_speed) * (
        wave_rows * wave_rows + wave_columns * wave_columns
    )
    inverse = lax.rsqrt(squared)
    inverse = inverse * (1.5 - 0.5 * squared * inverse * inverse)
    sine, cosine = sine_cosine(squared * inverse * phase_value)
    return sine * inverse, (1.0 - cosine) * (inverse * inverse)


def wave_operator(fields, speed_rows, speed_columns):
    east_r, east_i, north_r, north_i, height_r, height_i = fields
    return (
        coriolis * north_r + speed_rows * height_i,
        coriolis * north_i - speed_rows * height_r,
        speed_columns * height_i - coriolis * east_r,
        -speed_columns * height_r - coriolis * east_i,
        speed_rows * east_i + speed_columns * north_i,
        -(speed_rows * east_r + speed_columns * north_r),
    )


def wave_exponential(fields, wave_rows, wave_columns, sine_term, cosine_term):
    speed_rows = wave_speed * wave_rows
    speed_columns = wave_speed * wave_columns
    single = wave_operator(fields, speed_rows, speed_columns)
    double = wave_operator(single, speed_rows, speed_columns)
    return [w + sine_term * a + cosine_term * b for w, a, b in zip(fields, single, double)]


def lanes_of(rows):
    return lax.broadcasted_iota(jnp.int32, (rows, LANES), 1)


def roll(values, shift):
    return pltpu.roll(values, shift % LANES, 1)


def swap_blocks(parts, width):
    parts = list(parts)
    lane = lanes_of(parts[0].shape[0])
    step = 1
    while step < len(parts):
        shift = width * step
        odd = (lane & shift) == shift
        for low in range(len(parts)):
            if low & step:
                continue
            high = low | step
            parts[low], parts[high] = (
                jnp.where(odd, roll(parts[high], shift), parts[low]),
                jnp.where(odd, parts[high], roll(parts[low], -shift)),
            )
        step *= 2
    return parts


def own_columns(rows):
    device = (lax.axis_index("xy") * 2 + lax.axis_index("c")) * 4
    device = device + lax.axis_index("zm") * 2 + lax.axis_index("yh")
    return wave_of(lax.broadcasted_iota(jnp.int32, (rows, LANES), 0) + device * LINES)


def spread_kernel(state_ref, out_ref):
    def plane(index):
        return state_ref[index // 2, index % 2]

    left = jnp.concatenate([plane(index) for index in range(4)], axis=0)
    right = jnp.concatenate([plane(4), plane(5), jnp.zeros((64, 64), F32)], axis=0)
    turned = jnp.concatenate([left, right], axis=1).T
    low = lanes_of(8) < 64
    for part in range(4):
        main = turned[LINES * part : LINES * (part + 1)]
        rest = turned[64 + LINES * part : 64 + LINES * (part + 1)]
        rest = jnp.where(low, rest[:8], roll(rest[8:], 64))
        message = jnp.concatenate([main, rest], axis=0).astype(BF16)
        for block in range(8):
            out_ref[4 * block + part] = message


def first_kernel(settings_ref, gathered_ref, table_ref, out_ref, rotated):
    wave_columns = own_columns(LINES)
    for group in range(8):
        lanes = slice(LANES * group, LANES * (group + 1))
        messages = [gathered_ref[4 * group + offset].astype(F32) for offset in range(4)]
        planes = swap_blocks([message[:16] for message in messages], 32)
        rest = swap_blocks([message[16:] for message in messages], 32)
        planes.append(jnp.concatenate([rest[0], rest[2]], axis=0))
        planes.append(jnp.concatenate([rest[1], rest[3]], axis=0))
        wave_rows = wave_of(lanes_of(LINES) + LANES * group)
        for phase in range(2):
            phase_value = settings_ref[phase, 0].astype(F32) * phase_step
            terms = exponential_terms(wave_rows, wave_columns, phase_value)
            result = wave_exponential(planes, wave_rows, wave_columns, *terms)
            for plane in range(6):
                start = 96 * phase + LINES * plane
                rotated[start : start + LINES, lanes] = result[plane].astype(BF16)
    for chunk in range(4):
        columns = slice(256 * chunk, 256 * (chunk + 1))
        data = rotated[...]
        cosine = jnp.dot(data, table_ref[0, :, columns], preferred_element_type=F32)
        sine = jnp.dot(data, table_ref[1, :, columns], preferred_element_type=F32)
        for part in range(2):
            lanes = slice(LANES * part, LANES * (part + 1))
            real, imag = [], []
            for field in range(6):
                top = slice(32 * field, 32 * field + LINES)
                bottom = slice(32 * field + LINES, 32 * (field + 1))
                real.append(cosine[top, lanes] - sine[bottom, lanes])
                imag.append(sine[top, lanes] + cosine[bottom, lanes])
            main = swap_blocks(real + imag[:2], 16)
            rest = swap_blocks([v[:8] for v in imag[2:]] + [v[8:] for v in imag[2:]], 16)
            for offset in range(8):
                message = jnp.concatenate([main[offset], rest[offset]], axis=0)
                out_ref[8 * (2 * chunk + part) + offset] = message.astype(BF16)


def second_kernel(arrived_ref, table_ref, out_ref, real_part, imag_part, pairs):
    first = lanes_of(LINES) < 32
    for source in range(64):
        message = arrived_ref[source].astype(F32)
        main, rest = message[:16], message[16:]
        rest = jnp.concatenate([roll(rest, 32), roll(rest, -32)], axis=0)
        imag = jnp.where(first, roll(main, 32), rest)
        rows = slice(LINES * source, LINES * (source + 1))
        real_part[rows, :] = main.astype(BF16)
        imag_part[rows, :] = (-imag).astype(BF16)
    block = lanes_of(256) // 16
    height_lanes = (block == 2) | (block == 5)
    for chunk in range(4):
        rows = slice(256 * chunk, 256 * (chunk + 1))
        grid = jnp.dot(table_ref[0, rows, :], real_part[...], preferred_element_type=F32)
        grid = grid + jnp.dot(table_ref[1, rows, :], imag_part[...], preferred_element_type=F32)
        grid = grid * (1.0 / N)
        other = jnp.where(height_lanes, roll(grid, 32), grid)
        pairs[rows, :LANES] = (grid * other).astype(BF16)
        pairs[rows, LANES:] = (grid * roll(grid, 16)).astype(BF16)
    lane = lanes_of(LINES)
    short = lanes_of(8)
    for chunk in range(4):
        rows = slice(256 * chunk, 256 * (chunk + 1))
        real = jnp.dot(table_ref[0, rows, :], pairs[...], preferred_element_type=F32)
        imag = -jnp.dot(table_ref[1, rows, :], pairs[...], preferred_element_type=F32)
        for offset in range(16):
            own = slice(LINES * offset, LINES * (offset + 1))
            real_rest, imag_rest = real[own, LANES:], imag[own, LANES:]
            first_rows = jnp.where(lane < 96, real[own, :LANES], roll(real_rest, 80))
            second_rows = jnp.where(lane < 96, imag[own, :LANES], roll(imag_rest, 80))
            last_rows = jnp.where(
                short < 64,
                jnp.where(short < 32, roll(real_rest[:8], 64), roll(imag_rest[:8], -32)),
                jnp.where(short < 96, real_rest[8:], roll(imag_rest[8:], 32)),
            )
            message = jnp.concatenate([first_rows, second_rows, last_rows], axis=0)
            out_ref[16 * chunk + offset] = message.astype(BF16)


PRODUCT_ORDER = ((0, 0), (0, 2), (0, 3), (1, 0), (1, 2), (1, 3), (0, 1), (0, 4))


def third_kernel(settings_ref, returned_ref, table_ref, out_ref, lines):
    wave_columns = own_columns(LINES)
    for group in range(8):
        lanes = slice(LANES * group, LANES * (group + 1))
        messages = [returned_ref[8 * group + offset].astype(F32) for offset in range(8)]
        rest = swap_blocks([message[32:] for message in messages], 16)
        for part in range(2):
            blocks = swap_blocks([m[16 * part : 16 * (part + 1)] for m in messages], 16)
            places = list(PRODUCT_ORDER) + [(1, 1), (1, 4)]
            blocks.append(jnp.concatenate([rest[2 * part], rest[4 + 2 * part]], axis=0))
            blocks.append(jnp.concatenate([rest[2 * part + 1], rest[5 + 2 * part]], axis=0))
            for (phase, product), block in zip(places, blocks):
                start = 160 * part + 80 * phase + LINES * product
                lines[start : start + LINES, lanes] = block.astype(BF16)
    for chunk in range(4):
        columns = slice(256 * chunk, 256 * (chunk + 1))
        data = lines[...]
        cosine = jnp.dot(data, table_ref[0, :, columns], preferred_element_type=F32)
        sine = jnp.dot(data, table_ref[1, :, columns], preferred_element_type=F32)
        for part in range(2):
            lanes = slice(LANES * part, LANES * (part + 1))
            group = 2 * chunk + part
            wave_rows = wave_of(lanes_of(LINES) + LANES * group)
            total = None
            for phase in range(2):
                phase_value = settings_ref[phase, 0].astype(F32) * phase_step
                weight = settings_ref[phase, 1].astype(F32) * (1.0 / weight_scale)
                real, imag = [], []
                for product in range(5):
                    start = 80 * phase + LINES * product
                    top = slice(start, start + LINES)
                    bottom = slice(160 + start, 160 + start + LINES)
                    real.append((cosine[top, lanes] + sine[bottom, lanes]) * (1.0 / N))
                    imag.append((cosine[bottom, lanes] - sine[top, lanes]) * (1.0 / N))
                tendency = []
                for toward_east, toward_north in ((0, 1), (1, 2), (3, 4)):
                    tendency.append(wave_rows * imag[toward_east] + wave_columns * imag[toward_north])
                    tendency.append(
                        -(wave_rows * real[toward_east] + wave_columns * real[toward_north])
                    )
                sine_term, cosine_term = exponential_terms(wave_rows, wave_columns, phase_value)
                result = wave_exponential(
                    tendency, wave_rows, wave_columns, -sine_term, cosine_term
                )
                result = [weight * plane for plane in result]
                total = result if total is None else [a + b for a, b in zip(total, result)]
            main = swap_blocks(total[:4], 32)
            rest = swap_blocks([total[4][:8], total[5][:8], total[4][8:], total[5][8:]], 32)
            for offset in range(4):
                message = jnp.concatenate([main[offset], rest[offset]], axis=0)
                out_ref[4 * group + offset] = message.astype(BF16)


def last_kernel(state_ref, parts_ref, out_ref):
    mains, rests = [], []
    for part in range(4):
        total = parts_ref[part].astype(F32)
        for block in range(1, 8):
            total = total + parts_ref[4 * block + part].astype(F32)
        mains.append(total[:16])
        rests.append(jnp.concatenate([total[16:], roll(total[16:], 64)], axis=0))
    turned = jnp.concatenate(mains + rests, axis=0).T
    row_start = (lax.axis_index("zb") * 4 + lax.axis_index("zm") * 2 + lax.axis_index("yh")) * ROWS
    column_start = (lax.axis_index("xy") * 2 + lax.axis_index("c")) * 64
    wave_rows = wave_of(lax.broadcasted_iota(jnp.int32, (ROWS, 64), 0) + row_start)
    wave_columns = wave_of(lax.broadcasted_iota(jnp.int32, (ROWS, 64), 1) + column_start)
    fields = []
    for plane in range(6):
        rows = slice(ROWS * (plane % 4), ROWS * (plane % 4 + 1))
        total = turned[rows, :64] if plane < 4 else turned[rows, 64:]
        fields.append(state_ref[plane // 2, plane % 2] + time_step * total)
    terms = exponential_terms(wave_rows, wave_columns, time_step)
    result = wave_exponential(fields, wave_rows, wave_columns, *terms)
    for plane in range(6):
        out_ref[plane // 2, plane % 2] = result[plane]


def call(kernel, name, shape, dtype, scratch, places, flops):
    spots = [pl.BlockSpec(memory_space=pltpu.SMEM if p == "s" else pltpu.VMEM) for p in places]
    return pl.pallas_call(
        kernel,
        name=name,
        out_shape=jax.ShapeDtypeStruct(shape, dtype),
        in_specs=spots,
        out_specs=pl.BlockSpec(memory_space=pltpu.VMEM),
        scratch_shapes=[pltpu.VMEM(s, BF16) for s in scratch],
        cost_estimate=pl.CostEstimate(flops=flops, bytes_accessed=1 << 20, transcendentals=0),
        compiler_params=pltpu.CompilerParams(vmem_limit_bytes=VMEM_LIMIT),
    )


def per_device(spectral_state, phase_index, weight_count):
    tables = fourier_tables()
    settings = lax.all_gather(jnp.stack([phase_index, weight_count], axis=1), "c", axis=0, tiled=True)
    settings = lax.ppermute(
        settings, ("xy", "zb"), [(8 * i + j, 8 * j + i) for i in range(8) for j in range(8)]
    )
    spread = call(spread_kernel, "spread", (32, 24, LANES), BF16, [], "v", 1 << 33)(spectral_state)
    gathered = lax.all_to_all(spread, MAIN_AXES, 0, 0)
    outgoing = call(first_kernel, "inverse_rows", (64, 24, LANES), BF16, [(192, N)], "svv", 1 << 30)(
        settings, gathered, tables
    )
    arrived = lax.all_to_all(outgoing, GROUP_AXES, 0, 0)
    outgoing_back = call(
        second_kernel,
        "grid_products",
        (64, 40, LANES),
        BF16,
        [(N, LANES), (N, LANES), (N, 2 * LANES)],
        "vv",
        1 << 30,
    )(arrived, tables)
    returned = lax.all_to_all(outgoing_back, GROUP_AXES, 0, 0)
    weighted = call(third_kernel, "forward_rows", (32, 24, LANES), BF16, [(320, N)], "svv", 1 << 31)(
        settings, returned, tables
    )
    parts = lax.all_to_all(weighted, MAIN_AXES, 0, 0)
    return call(last_kernel, "advance", spectral_state.shape, F32, [], "vv", 1 << 24)(spectral_state, parts)


def solution(mesh):
    fine = Mesh(mesh.devices.reshape(8, 2, 8, 2, 2), ("xy", "c", "zb", "zm", "yh"))
    rows, columns = ("zb", "zm", "yh"), ("xy", "c")
    in_specs = (P(None, None, rows, columns), P(columns), P(columns))
    out_specs = P(None, None, rows, columns)
    return jax.shard_map(
        per_device, mesh=fine, in_specs=in_specs, out_specs=out_specs, check_vma=False
    )
```

time: 131 us -> 118 us (0.901)
  waiting for transfers between devices: 44.7 us -> 11.2 us
  blocking collectives: 57.1 us -> 69 us
  starting transfers between devices: 10.9 us -> 22.7 us
  local copies, waits for them, and re-layouts: 5.68 us -> 3.09 us
    all_to_all x2 -> x1, waiting for transfers between devices: 44.7 us -> 8.39 us  [per_device(): gathered = lax.all_to_all(spread, MAIN_AXES, 0, 0)]
    all_to_all x2 -> x3, blocking collectives: 57.1 us -> 67.2 us  [the longest x1 30 us: per_device(): parts = lax.all_to_all(weighted, MAIN_AXES, 0, 0)]
    all_to_all x2 -> x1, starting transfers between devices: 10.9 us -> 18.2 us  [per_device(): gathered = lax.all_to_all(spread, MAIN_AXES, 0, 0)]
    ppermute x0 -> x1, starting transfers between devices: none -> 4.44 us  [per_device(): lax.ppermute(settings, ('xy', 'zb'), [(8 * i + j, 8 * j + i) for i in ran...]
    ppermute x0 -> x1, waiting for transfers between devices: none -> 2.8 us  [per_device(): lax.ppermute(settings, ('xy', 'zb'), [(8 * i + j, 8 * j + i) for i in ran...]
    unnamed x14 -> x8, local copies, waits for them, and re-layouts: 5.68 us -> 3.09 us
    all_gather x0 -> x1, blocking collectives: none -> 1.75 us  [per_device(): lax.all_gather(jnp.stack([phase_index, weight_count], axis=1), 'c', axis=...]
where the time goes in v1:
time: 118 us; the launch traced here: 117 us
  blocking collectives  69 us (58%)
  starting transfers between devices  22.7 us (19%)
  waiting for transfers between devices  11.2 us (9%)
  Pallas kernels  10.1 us (9%)
  local copies, waits for them, and re-layouts  3.09 us (3%)
  between operations  1.34 us (1%)
    all_to_all x1, blocking collectives, per_device(): parts = lax.all_to_all(weighted, MAIN_AXES, 0, 0)  30 us
    all_to_all x1, blocking collectives, per_device(): arrived = lax.all_to_all(outgoing, GROUP_AXES, 0, 0)  19.2 us
    all_to_all x1, starting transfers between devices, per_device(): gathered = lax.all_to_all(spread, MAIN_AXES, 0, 0)  18.2 us
    all_to_all x1, blocking collectives, per_device(): returned = lax.all_to_all(outgoing_back, GROUP_AXES, 0, 0)  18 us
    all_to_all x1, waiting for transfers between devices, per_device(): gathered = lax.all_to_all(spread, MAIN_AXES, 0, 0)  8.39 us
    ppermute x1, starting transfers between devices, per_device(): lax.ppermute(settings, ('xy', 'zb'), [(8 * i + j, 8 * j + i) for i in ran...  4.44 us
    pallas_call x1, Pallas kernels, per_device(): call(third_kernel, 'forward_rows', (32, 24, LANES), BF16, [(320, N)], 'sv...  3.34 us
    unnamed x8, local copies, waits for them, and re-layouts  3.09 us
  transfers between devices with their start and end apart: 2, of which 2 were waited for; matrix products, arithmetic and copies ran while one was open for 0% of the time, Pallas kernels for 0%

profile of v1, /device:TPU:24, one launch (start us, length us, event | category | flops | bytes accessed | tf_op | source)
XLA Modules:
  0.0 117.4 jit_solution(3527014904057794369)
XLA Ops:
  0.0 0.0 copy-start.2
  0.0 0.9 copy-done.2
  0.9 0.9 spread.1
  1.8 18.2 %all-to-all-start = ((bf16[32,24,128]{2,1,0:T(8,128)(2,1)}), bf16[32,24,128]{2,1,0:T(8,128)(2,1)S(1)}, u32[]{:S(2)}, u32[]{:S(2)}) async-start(bf16[32,24,128]{2,1,0:T(8,128)(2,1)} %spread.1), calls=%async_computation | async-start | bytes 393216 | tf_op jit(solution)/shard_map/all_to_all | solution.py:317
  21.3 0.1 add_bitcast_fusion
  21.4 1.8 %all-gather = s32[2,1,2]{2,1,0:T(1,128)S(1)} all-gather(s32[1,1,2]{2,1,0:T(1,128)S(1)} %add_bitcast_fusion), channel_id=1, replica_groups=mesh['xy'=8,'c'=2,'zb'=8,'zm'=2,'yh'=2] {'c'}, dimensions={0}, use_global_device_ids=true | all-gather | bytes 24 | tf_op jit(solution)/shard_map/all_gather | solution.py:312
  23.1 4.4 %collective-permute-start = (s32[2,2]{1,0:T(2,128)S(1)}, s32[2,2]{1,0:T(2,128)S(1)}, u32[]{:S(2)}, u32[]{:S(2)}) collective-permute-start(s32[2,2]{1,0:T(2,128)S(1)} %bitcast.7), channel_id=1, source_target_pairs={{0,0},{4,64},{8,128},{12,192},{16,256},{20,320},{24,384},{28,448},... | collective-permute-start | bytes 56 | tf_op jit(solution)/shard_map/ppermute | solution.py:313
  27.6 2.8 %collective-permute-done.settings_ref = s32[2,2]{1,0:T(2,128)S(1)} collective-permute-done((s32[2,2]{1,0:T(2,128)S(1)}, s32[2,2]{1,0:T(2,128)S(1)}, u32[]{:S(2)}, u32[]{:S(2)}) %collective-permute-start) | collective-permute-done | bytes 48 | tf_op jit(solution)/shard_map/ppermute | solution.py:313
  30.4 8.4 %all-to-all-done.gathered_ref = bf16[32,24,128]{2,1,0:T(8,128)(2,1)S(1)} async-done(((bf16[32,24,128]{2,1,0:T(8,128)(2,1)}), bf16[32,24,128]{2,1,0:T(8,128)(2,1)S(1)}, u32[]{:S(2)}, u32[]{:S(2)}) %all-to-all-start) | async-done | bytes 196640 | tf_op jit(solution)/shard_map/all_to_all | solution.py:317
  38.8 0.0 copy-start
  38.8 2.2 %copy-done = bf16[2,1024,1024]{2,1,0:T(8,128)(2,1)S(1)} copy-done((bf16[2,1024,1024]{2,1,0:T(8,128)(2,1)S(1)}, bf16[2,1024,1024]{2,1,0:T(8,128)(2,1)}, u32[]{:S(2)}) %copy-start) | copy-done | bytes 4194328
  41.0 0.0 copy-start.1
  41.0 2.4 %inverse_rows.1 = bf16[64,24,128]{2,1,0:T(8,128)(2,1)S(1)} custom-call(s32[2,2]{1,0:T(2,128)S(1)} %collective-permute-done.settings_ref, bf16[32,24,128]{2,1,0:T(8,128)(2,1)S(1)} %all-to-all-done.gathered_ref, bf16[2,1024,1024]{2,1,0:T(8,128)(2,1)S(1)} %copy-done), custom_call_target="tpu_custom_call" | custom-call | flops 1073741824 | bytes 1048576 | tf_op jit(solution)/shard_map/inverse_rows/pallas_call | solution.py:318
  43.3 19.2 %all_to_all.20.arrived_ref = bf16[64,24,128]{2,1,0:T(8,128)(2,1)S(1)} all-to-all(bf16[64,24,128]{2,1,0:T(8,128)(2,1)S(1)} %inverse_rows.1), channel_id=1, replica_groups=mesh['xy'=8,'c'=2,'zb'=8,'zm'=2,'yh'=2] {'xy','c','zm','yh'}, dimensions={0} | all-to-all | bytes 786432 | tf_op jit(solution)/shard_map/all_to_all | solution.py:321
  62.6 0.0 copy-done.1
  62.6 2.6 %grid_products.1 = bf16[64,40,128]{2,1,0:T(8,128)(2,1)S(1)} custom-call(bf16[64,24,128]{2,1,0:T(8,128)(2,1)S(1)} %all_to_all.20.arrived_ref, bf16[2,1024,1024]{2,1,0:T(8,128)(2,1)S(1)} %copy-done.1), custom_call_target="tpu_custom_call" | custom-call | flops 1073741824 | bytes 1048576 | tf_op jit(solution)/shard_map/grid_products/pallas_call | solution.py:322
  65.2 18.0 %all_to_all.21.returned_ref = bf16[64,40,128]{2,1,0:T(8,128)(2,1)S(1)} all-to-all(bf16[64,40,128]{2,1,0:T(8,128)(2,1)S(1)} %grid_products.1), channel_id=1, replica_groups=mesh['xy'=8,'c'=2,'zb'=8,'zm'=2,'yh'=2] {'xy','c','zm','yh'}, dimensions={0} | all-to-all | bytes 1310720 | tf_op jit(solution)/shard_map/all_to_all | solution.py:331
  83.2 0.0 copy-start.3
  83.2 3.3 %forward_rows.1 = bf16[32,24,128]{2,1,0:T(8,128)(2,1)S(1)} custom-call(s32[2,2]{1,0:T(2,128)S(1)} %collective-permute-done.settings_ref, bf16[64,40,128]{2,1,0:T(8,128)(2,1)S(1)} %all_to_all.21.returned_ref, bf16[2,1024,1024]{2,1,0:T(8,128)(2,1)S(1)} %copy-done.1), custom_call_target="tpu_custom_call" | custom-call | flops 2147483648 | bytes 1048576 | tf_op jit(solution)/shard_map/forward_rows/pallas_call | solution.py:332
  86.5 30.0 %all_to_all.22.parts_ref = bf16[32,24,128]{2,1,0:T(8,128)(2,1)S(1)} all-to-all(bf16[32,24,128]{2,1,0:T(8,128)(2,1)S(1)} %forward_rows.1), channel_id=1, replica_groups=mesh['xy'=8,'c'=2,'zb'=8,'zm'=2,'yh'=2] {'zb','zm','yh'}, dimensions={0} | all-to-all | bytes 393216 | tf_op jit(solution)/shard_map/all_to_all | solution.py:335
  116.5 0.0 copy-done.3
  116.5 0.9 advance.1
Async XLA Ops:
  0.0 0.9 copy-start.2
  1.8 37.0 %all-to-all-start = ((bf16[32,24,128]{2,1,0:T(8,128)(2,1)}), bf16[32,24,128]{2,1,0:T(8,128)(2,1)S(1)}, u32[]{:S(2)}, u32[]{:S(2)}) async-start(bf16[32,24,128]{2,1,0:T(8,128)(2,1)} %spread.1), calls=%async_computation | async-start | bytes 393216 | tf_op jit(solution)/shard_map/all_to_all | solution.py:317
  23.1 7.2 %collective-permute-start = (s32[2,2]{1,0:T(2,128)S(1)}, s32[2,2]{1,0:T(2,128)S(1)}, u32[]{:S(2)}, u32[]{:S(2)}) collective-permute-start(s32[2,2]{1,0:T(2,128)S(1)} %bitcast.7), channel_id=1, source_target_pairs={{0,0},{4,64},{8,128},{12,192},{16,256},{20,320},{24,384},{28,448},... | collective-permute-start | bytes 56 | tf_op jit(solution)/shard_map/ppermute | solution.py:313
  38.8 2.2 %copy-start = (bf16[2,1024,1024]{2,1,0:T(8,128)(2,1)S(1)}, bf16[2,1024,1024]{2,1,0:T(8,128)(2,1)}, u32[]{:S(2)}) copy-start(bf16[2,1024,1024]{2,1,0:T(8,128)(2,1)} %constant.2.clone.table_ref) | copy-start | bytes 12582916
  41.0 21.6 %copy-start.1 = (bf16[2,1024,1024]{2,1,0:T(8,128)(2,1)S(1)}, bf16[2,1024,1024]{2,1,0:T(8,128)(2,1)}, u32[]{:S(2)}) copy-start(bf16[2,1024,1024]{2,1,0:T(8,128)(2,1)} %constant.2.clone.table_ref) | copy-start | bytes 12582916
  83.2 33.3 %copy-start.3 = (f32[3,2,32,64]{3,2,1,0:T(8,128)S(1)}, f32[3,2,32,64]{3,2,1,0:T(8,128)}, u32[]{:S(2)}) copy-start(f32[3,2,32,64]{3,2,1,0:T(8,128)} %state_ref.3) | copy-start | bytes 147460

commit v2 on v1

--- a/solution.py
+++ b/solution.py
@@ -23,14 +23,15 @@
 VMEM_LIMIT = 28 * 1024 * 1024
 F32 = jnp.float32
 BF16 = jnp.bfloat16
-MAIN_AXES = ("zb", "zm", "yh")
+MAIN_AXES = ("zl", "zm", "zh", "yh")
 GROUP_AXES = ("xy", "c", "zm", "yh")
 
 
 def fourier_tables():
-    positions = np.arange(N, dtype=np.int64)
-    angles = (positions[:, None] * positions[None, :] % N).astype(np.float64) * (2.0 * math.pi / N)
-    return jnp.asarray(np.stack([np.cos(angles), np.sin(angles)]), BF16)
+    product = np.arange(N)[:, None] * np.arange(N // 2)[None, :] % N
+    angles = product.astype(np.float64) * (2.0 * math.pi / N)
+    tables = np.stack([np.cos(angles), np.sin(angles)])
+    return jnp.asarray(tables, BF16), jnp.asarray(tables.transpose(0, 2, 1), BF16)
 
 
 def wave_of(index):
@@ -113,13 +114,31 @@
     return parts
 
 
+def slot(device):
+    high, low, rest = device // 16, device // 4 % 4, device % 4
+    return low * 8 + rest // 2 * 4 + high * 2 + rest % 2
+
+
+def own_block():
+    return 4 * lax.axis_index("zh") + lax.axis_index("zl")
+
+
+def alternate(values, axis):
+    index = lax.broadcasted_iota(jnp.int32, values.shape, axis)
+    return jnp.where((index & 1) == 1, -values, values)
+
+
 def own_columns(rows):
     device = (lax.axis_index("xy") * 2 + lax.axis_index("c")) * 4
     device = device + lax.axis_index("zm") * 2 + lax.axis_index("yh")
     return wave_of(lax.broadcasted_iota(jnp.int32, (rows, LANES), 0) + device * LINES)
 
 
-def spread_kernel(state_ref, out_ref):
+def spread_kernel(phase_ref, weight_ref, state_ref, out_ref, settings_ref):
+    phase_value = phase_ref[0].astype(F32) * phase_step
+    weight = weight_ref[0].astype(F32) * (1.0 / weight_scale)
+    settings_ref[...] = jnp.where(lanes_of(8) < 64, phase_value, weight)
+
     def plane(index):
         return state_ref[index // 2, index % 2]
 
@@ -133,44 +152,48 @@
         rest = jnp.where(low, rest[:8], roll(rest[8:], 64))
         message = jnp.concatenate([main, rest], axis=0).astype(BF16)
         for block in range(8):
-            out_ref[4 * block + part] = message
+            out_ref[slot(4 * block + part)] = message
 
 
 def first_kernel(settings_ref, gathered_ref, table_ref, out_ref, rotated):
     wave_columns = own_columns(LINES)
     for group in range(8):
         lanes = slice(LANES * group, LANES * (group + 1))
-        messages = [gathered_ref[4 * group + offset].astype(F32) for offset in range(4)]
+        messages = [gathered_ref[slot(4 * group + offset)].astype(F32) for offset in range(4)]
         planes = swap_blocks([message[:16] for message in messages], 32)
         rest = swap_blocks([message[16:] for message in messages], 32)
         planes.append(jnp.concatenate([rest[0], rest[2]], axis=0))
         planes.append(jnp.concatenate([rest[1], rest[3]], axis=0))
         wave_rows = wave_of(lanes_of(LINES) + LANES * group)
         for phase in range(2):
-            phase_value = settings_ref[phase, 0].astype(F32) * phase_step
+            phase_value = settings_ref[phase, :1, :1]
             terms = exponential_terms(wave_rows, wave_columns, phase_value)
             result = wave_exponential(planes, wave_rows, wave_columns, *terms)
             for plane in range(6):
                 start = 96 * phase + LINES * plane
                 rotated[start : start + LINES, lanes] = result[plane].astype(BF16)
-    for chunk in range(4):
+                start = start + 192
+                rotated[start : start + LINES, lanes] = alternate(result[plane], 1).astype(BF16)
+    for chunk in range(2):
         columns = slice(256 * chunk, 256 * (chunk + 1))
         data = rotated[...]
         cosine = jnp.dot(data, table_ref[0, :, columns], preferred_element_type=F32)
         sine = jnp.dot(data, table_ref[1, :, columns], preferred_element_type=F32)
-        for part in range(2):
-            lanes = slice(LANES * part, LANES * (part + 1))
+        for part in range(4):
+            lanes = slice(LANES * (part % 2), LANES * (part % 2 + 1))
+            group = 4 * (part // 2) + 2 * chunk + part % 2
             real, imag = [], []
             for field in range(6):
-                top = slice(32 * field, 32 * field + LINES)
-                bottom = slice(32 * field + LINES, 32 * (field + 1))
+                start = 192 * (part // 2) + 32 * field
+                top = slice(start, start + LINES)
+                bottom = slice(start + LINES, start + 2 * LINES)
                 real.append(cosine[top, lanes] - sine[bottom, lanes])
                 imag.append(sine[top, lanes] + cosine[bottom, lanes])
             main = swap_blocks(real + imag[:2], 16)
             rest = swap_blocks([v[:8] for v in imag[2:]] + [v[8:] for v in imag[2:]], 16)
             for offset in range(8):
                 message = jnp.concatenate([main[offset], rest[offset]], axis=0)
-                out_ref[8 * (2 * chunk + part) + offset] = message.astype(BF16)
+                out_ref[8 * group + offset] = message.astype(BF16)
 
 
 def second_kernel(arrived_ref, table_ref, out_ref, real_part, imag_part, pairs):
@@ -181,36 +204,47 @@
         rest = jnp.concatenate([roll(rest, 32), roll(rest, -32)], axis=0)
         imag = jnp.where(first, roll(main, 32), rest)
         rows = slice(LINES * source, LINES * (source + 1))
-        real_part[rows, :] = main.astype(BF16)
-        imag_part[rows, :] = (-imag).astype(BF16)
+        real_part[rows, :LANES] = main.astype(BF16)
+        real_part[rows, LANES:] = alternate(main, 0).astype(BF16)
+        imag_part[rows, :LANES] = (-imag).astype(BF16)
+        imag_part[rows, LANES:] = alternate(-imag, 0).astype(BF16)
     block = lanes_of(256) // 16
     height_lanes = (block == 2) | (block == 5)
-    for chunk in range(4):
+    for chunk in range(2):
         rows = slice(256 * chunk, 256 * (chunk + 1))
         grid = jnp.dot(table_ref[0, rows, :], real_part[...], preferred_element_type=F32)
         grid = grid + jnp.dot(table_ref[1, rows, :], imag_part[...], preferred_element_type=F32)
         grid = grid * (1.0 / N)
-        other = jnp.where(height_lanes, roll(grid, 32), grid)
-        pairs[rows, :LANES] = (grid * other).astype(BF16)
-        pairs[rows, LANES:] = (grid * roll(grid, 16)).astype(BF16)
+        for upper in range(2):
+            part = grid[:, LANES * upper : LANES * (upper + 1)]
+            target = slice(512 * upper + 256 * chunk, 512 * upper + 256 * (chunk + 1))
+            other = jnp.where(height_lanes, roll(part, 32), part)
+            for place, product in enumerate((part * other, part * roll(part, 16))):
+                lanes = slice(LANES * place, LANES * (place + 1))
+                pairs[target, lanes] = product.astype(BF16)
+                lanes = slice(LANES * (place + 2), LANES * (place + 3))
+                pairs[target, lanes] = alternate(product, 0).astype(BF16)
     lane = lanes_of(LINES)
     short = lanes_of(8)
-    for chunk in range(4):
+    for chunk in range(2):
         rows = slice(256 * chunk, 256 * (chunk + 1))
         real = jnp.dot(table_ref[0, rows, :], pairs[...], preferred_element_type=F32)
         imag = -jnp.dot(table_ref[1, rows, :], pairs[...], preferred_element_type=F32)
-        for offset in range(16):
+        for index in range(32):
+            upper, offset = index // 16, index % 16
             own = slice(LINES * offset, LINES * (offset + 1))
-            real_rest, imag_rest = real[own, LANES:], imag[own, LANES:]
-            first_rows = jnp.where(lane < 96, real[own, :LANES], roll(real_rest, 80))
-            second_rows = jnp.where(lane < 96, imag[own, :LANES], roll(imag_rest, 80))
+            main = slice(256 * upper, 256 * upper + LANES)
+            rest = slice(256 * upper + LANES, 256 * (upper + 1))
+            real_rest, imag_rest = real[own, rest], imag[own, rest]
+            first_rows = jnp.where(lane < 96, real[own, main], roll(real_rest, 80))
+            second_rows = jnp.where(lane < 96, imag[own, main], roll(imag_rest, 80))
             last_rows = jnp.where(
                 short < 64,
                 jnp.where(short < 32, roll(real_rest[:8], 64), roll(imag_rest[:8], -32)),
                 jnp.where(short < 96, real_rest[8:], roll(imag_rest[8:], 32)),
             )
             message = jnp.concatenate([first_rows, second_rows, last_rows], axis=0)
-            out_ref[16 * chunk + offset] = message.astype(BF16)
+            out_ref[32 * upper + 16 * chunk + offset] = message.astype(BF16)
 
 
 PRODUCT_ORDER = ((0, 0), (0, 2), (0, 3), (1, 0), (1, 2), (1, 3), (0, 1), (0, 4))
@@ -230,22 +264,24 @@
             for (phase, product), block in zip(places, blocks):
                 start = 160 * part + 80 * phase + LINES * product
                 lines[start : start + LINES, lanes] = block.astype(BF16)
-    for chunk in range(4):
+                start = start + 320
+                lines[start : start + LINES, lanes] = alternate(block, 1).astype(BF16)
+    for chunk in range(2):
         columns = slice(256 * chunk, 256 * (chunk + 1))
         data = lines[...]
         cosine = jnp.dot(data, table_ref[0, :, columns], preferred_element_type=F32)
         sine = jnp.dot(data, table_ref[1, :, columns], preferred_element_type=F32)
-        for part in range(2):
-            lanes = slice(LANES * part, LANES * (part + 1))
-            group = 2 * chunk + part
+        for part in range(4):
+            lanes = slice(LANES * (part % 2), LANES * (part % 2 + 1))
+            group = 4 * (part // 2) + 2 * chunk + part % 2
             wave_rows = wave_of(lanes_of(LINES) + LANES * group)
             total = None
             for phase in range(2):
-                phase_value = settings_ref[phase, 0].astype(F32) * phase_step
-                weight = settings_ref[phase, 1].astype(F32) * (1.0 / weight_scale)
+                phase_value = settings_ref[phase, :1, :1]
+                weight = settings_ref[phase, :1, 64:65]
                 real, imag = [], []
                 for product in range(5):
-                    start = 80 * phase + LINES * product
+                    start = 320 * (part // 2) + 80 * phase + LINES * product
                     top = slice(start, start + LINES)
                     bottom = slice(160 + start, 160 + start + LINES)
                     real.append((cosine[top, lanes] + sine[bottom, lanes]) * (1.0 / N))
@@ -266,19 +302,19 @@
             rest = swap_blocks([total[4][:8], total[5][:8], total[4][8:], total[5][8:]], 32)
             for offset in range(4):
                 message = jnp.concatenate([main[offset], rest[offset]], axis=0)
-                out_ref[4 * group + offset] = message.astype(BF16)
+                out_ref[slot(4 * group + offset)] = message.astype(BF16)
 
 
 def last_kernel(state_ref, parts_ref, out_ref):
     mains, rests = [], []
     for part in range(4):
-        total = parts_ref[part].astype(F32)
+        total = parts_ref[slot(part)].astype(F32)
         for block in range(1, 8):
-            total = total + parts_ref[4 * block + part].astype(F32)
+            total = total + parts_ref[slot(4 * block + part)].astype(F32)
         mains.append(total[:16])
         rests.append(jnp.concatenate([total[16:], roll(total[16:], 64)], axis=0))
     turned = jnp.concatenate(mains + rests, axis=0).T
-    row_start = (lax.axis_index("zb") * 4 + lax.axis_index("zm") * 2 + lax.axis_index("yh")) * ROWS
+    row_start = (own_block() * 4 + lax.axis_index("zm") * 2 + lax.axis_index("yh")) * ROWS
     column_start = (lax.axis_index("xy") * 2 + lax.axis_index("c")) * 64
     wave_rows = wave_of(lax.broadcasted_iota(jnp.int32, (ROWS, 64), 0) + row_start)
     wave_columns = wave_of(lax.broadcasted_iota(jnp.int32, (ROWS, 64), 1) + column_start)
@@ -293,14 +329,17 @@
         out_ref[plane // 2, plane % 2] = result[plane]
 
 
-def call(kernel, name, shape, dtype, scratch, places, flops):
+def call(kernel, name, shape, dtype, scratch, places, flops, outs=None):
     spots = [pl.BlockSpec(memory_space=pltpu.SMEM if p == "s" else pltpu.VMEM) for p in places]
+    whole = pl.BlockSpec(memory_space=pltpu.VMEM)
+    shapes = jax.ShapeDtypeStruct(shape, dtype)
+    extra = jax.ShapeDtypeStruct((8, LANES), F32)
     return pl.pallas_call(
         kernel,
         name=name,
-        out_shape=jax.ShapeDtypeStruct(shape, dtype),
+        out_shape=(shapes, extra) if outs else shapes,
         in_specs=spots,
-        out_specs=pl.BlockSpec(memory_space=pltpu.VMEM),
+        out_specs=(whole, whole) if outs else whole,
         scratch_shapes=[pltpu.VMEM(s, BF16) for s in scratch],
         cost_estimate=pl.CostEstimate(flops=flops, bytes_accessed=1 << 20, transcendentals=0),
         compiler_params=pltpu.CompilerParams(vmem_limit_bytes=VMEM_LIMIT),
@@ -308,14 +347,16 @@
 
 
 def per_device(spectral_state, phase_index, weight_count):
-    tables = fourier_tables()
-    settings = lax.all_gather(jnp.stack([phase_index, weight_count], axis=1), "c", axis=0, tiled=True)
+    tables, turned_tables = fourier_tables()
+    spread, settings = call(
+        spread_kernel, "spread", (32, 24, LANES), BF16, [], "ssv", 1 << 33, True
+    )(phase_index, weight_count, spectral_state)
+    settings = lax.all_gather(settings, "c")
     settings = lax.ppermute(
-        settings, ("xy", "zb"), [(8 * i + j, 8 * j + i) for i in range(8) for j in range(8)]
-    )
-    spread = call(spread_kernel, "spread", (32, 24, LANES), BF16, [], "v", 1 << 33)(spectral_state)
+        settings, ("xy", "zh", "zl"), [(8 * i + j, 8 * j + i) for i in range(8) for j in range(8)]
+    )
     gathered = lax.all_to_all(spread, MAIN_AXES, 0, 0)
-    outgoing = call(first_kernel, "inverse_rows", (64, 24, LANES), BF16, [(192, N)], "svv", 1 << 30)(
+    outgoing = call(first_kernel, "inverse_rows", (64, 24, LANES), BF16, [(384, N)], "vvv", 1 << 30)(
         settings, gathered, tables
     )
     arrived = lax.all_to_all(outgoing, GROUP_AXES, 0, 0)
@@ -324,12 +365,12 @@
         "grid_products",
         (64, 40, LANES),
         BF16,
-        [(N, LANES), (N, LANES), (N, 2 * LANES)],
+        [(N, 2 * LANES), (N, 2 * LANES), (N, 4 * LANES)],
         "vv",
         1 << 30,
-    )(arrived, tables)
+    )(arrived, turned_tables)
     returned = lax.all_to_all(outgoing_back, GROUP_AXES, 0, 0)
-    weighted = call(third_kernel, "forward_rows", (32, 24, LANES), BF16, [(320, N)], "svv", 1 << 31)(
+    weighted = call(third_kernel, "forward_rows", (32, 24, LANES), BF16, [(640, N)], "vvv", 1 << 31)(
         settings, returned, tables
     )
     parts = lax.all_to_all(weighted, MAIN_AXES, 0, 0)
@@ -337,8 +378,8 @@
 
 
 def solution(mesh):
-    fine = Mesh(mesh.devices.reshape(8, 2, 8, 2, 2), ("xy", "c", "zb", "zm", "yh"))
-    rows, columns = ("zb", "zm", "yh"), ("xy", "c")
+    fine = Mesh(mesh.devices.reshape(8, 2, 2, 4, 2, 2), ("xy", "c", "zh", "zl", "zm", "yh"))
+    rows, columns = ("zh", "zl", "zm", "yh"), ("xy", "c")
     in_specs = (P(None, None, rows, columns), P(columns), P(columns))
     out_specs = P(None, None, rows, columns)
     return jax.shard_map(

time: 118 us -> 113 us (0.958)
  local copies, waits for them, and re-layouts: 3.09 us -> 0.9 us
  blocking collectives: 69 us -> 67.7 us
  Pallas kernels: 10.1 us -> 8.89 us
    unnamed x8, local copies, waits for them, and re-layouts: 3.09 us -> 0.9 us
    all_to_all x1, blocking collectives: 30 us -> 27.8 us  [per_device(): parts = lax.all_to_all(weighted, MAIN_AXES, 0, 0)]
    all_to_all x1, waiting for transfers between devices: 8.39 us -> 7.1 us  [per_device(): gathered = lax.all_to_all(spread, MAIN_AXES, 0, 0)]
where the time goes in v2:
time: 113 us; the launch traced here: 112 us
  blocking collectives  67.7 us (60%)
  starting transfers between devices  22.7 us (20%)
  waiting for transfers between devices  10.4 us (9%)
  Pallas kernels  8.89 us (8%)
  between operations  1.35 us (1%)
    all_to_all x1, blocking collectives, per_device(): parts = lax.all_to_all(weighted, MAIN_AXES, 0, 0)  27.8 us
    all_to_all x1, blocking collectives, per_device(): arrived = lax.all_to_all(outgoing, GROUP_AXES, 0, 0)  20.1 us
    all_to_all x1, starting transfers between devices, per_device(): gathered = lax.all_to_all(spread, MAIN_AXES, 0, 0)  18.2 us
    all_to_all x1, blocking collectives, per_device(): returned = lax.all_to_all(outgoing_back, GROUP_AXES, 0, 0)  18 us
    all_to_all x1, waiting for transfers between devices, per_device(): gathered = lax.all_to_all(spread, MAIN_AXES, 0, 0)  7.1 us
    ppermute x1, starting transfers between devices, per_device(): lax.ppermute(settings, ('xy', 'zh', 'zl'), [(8 * i + j, 8 * j + i) for i...  4.44 us
    ppermute x1, waiting for transfers between devices, per_device(): lax.ppermute(settings, ('xy', 'zh', 'zl'), [(8 * i + j, 8 * j + i) for i...  3.34 us
    pallas_call x1, Pallas kernels, per_device(): call(third_kernel, 'forward_rows', (32, 24, LANES), BF16, [(640, N)], 'vv...  2.97 us
  transfers between devices with their start and end apart: 2, of which 2 were waited for; matrix products, arithmetic and copies ran while one was open for 0% of the time, Pallas kernels for 0%

profile of v2, /device:TPU:24, one launch (start us, length us, event | category | flops | bytes accessed | tf_op | source)
XLA Modules:
  0.0 112.0 jit_solution(16389464840291116801)
XLA Ops:
  1.3 0.0 copy-start
  1.3 0.9 copy-done
  2.2 0.0 copy-start.2
  2.2 0.9 spread.1
  3.1 18.2 %all-to-all-start = ((bf16[32,24,128]{2,1,0:T(8,128)(2,1)}), bf16[32,24,128]{2,1,0:T(8,128)(2,1)S(1)}, u32[]{:S(2)}, u32[]{:S(2)}) async-start(bf16[32,24,128]{2,1,0:T(8,128)(2,1)} %get-tuple-element.8), calls=%async_computation | async-start | bytes 393216 | tf_op jit(solution)/shard_map/all_to_all | solution.py:358
  21.3 1.8 %all-gather = f32[16,128]{1,0:T(8,128)S(1)} all-gather(f32[8,128]{1,0:T(8,128)S(1)} %get-tuple-element.7), channel_id=2, replica_groups=mesh['xy'=8,'c'=2,'zh'=2,'zl'=4,'zm'=2,'yh'=2] {'c'}, dimensions={0}, use_global_device_ids=true | all-gather | bytes 12288 | tf_op jit(solution)/shard_map/all_gather | solution.py:354
  23.1 4.4 %collective-permute-start = (f32[2,8,128]{2,1,0:T(8,128)S(1)}, f32[2,8,128]{2,1,0:T(8,128)S(1)}, u32[]{:S(2)}, u32[]{:S(2)}) collective-permute-start(f32[2,8,128]{2,1,0:T(8,128)S(1)} %bitcast.1), channel_id=1, source_target_pairs={{0,0},{4,64},{8,128},{12,192},{16,256},{20,320},{24,384},{28,448},... | collective-permute-start | bytes 24584 | tf_op jit(solution)/shard_map/ppermute | solution.py:355
  27.6 3.3 %collective-permute-done.settings_ref = f32[2,8,128]{2,1,0:T(8,128)S(1)} collective-permute-done((f32[2,8,128]{2,1,0:T(8,128)S(1)}, f32[2,8,128]{2,1,0:T(8,128)S(1)}, u32[]{:S(2)}, u32[]{:S(2)}) %collective-permute-start) | collective-permute-done | bytes 8224 | tf_op jit(solution)/shard_map/ppermute | solution.py:355
  30.9 7.1 %all-to-all-done.gathered_ref = bf16[32,24,128]{2,1,0:T(8,128)(2,1)S(1)} async-done(((bf16[32,24,128]{2,1,0:T(8,128)(2,1)}), bf16[32,24,128]{2,1,0:T(8,128)(2,1)S(1)}, u32[]{:S(2)}, u32[]{:S(2)}) %all-to-all-start) | async-done | bytes 196640 | tf_op jit(solution)/shard_map/all_to_all | solution.py:358
  38.0 0.0 copy-done.2
  38.0 0.0 copy-start.3
  38.0 1.8 %inverse_rows.1 = bf16[64,24,128]{2,1,0:T(8,128)(2,1)S(1)} custom-call(f32[2,8,128]{2,1,0:T(8,128)S(1)} %collective-permute-done.settings_ref, bf16[32,24,128]{2,1,0:T(8,128)(2,1)S(1)} %all-to-all-done.gathered_ref, bf16[2,1024,512]{2,1,0:T(8,128)(2,1)S(1)} %copy-done.2), custom_call_target="tpu_custom_call" | custom-call | flops 1073741824 | bytes 1048576 | tf_op jit(solution)/shard_map/inverse_rows/pallas_call | solution.py:359
  39.8 20.1 %all_to_all.20.arrived_ref = bf16[64,24,128]{2,1,0:T(8,128)(2,1)S(1)} all-to-all(bf16[64,24,128]{2,1,0:T(8,128)(2,1)S(1)} %inverse_rows.1), channel_id=1, replica_groups=mesh['xy'=8,'c'=2,'zh'=2,'zl'=4,'zm'=2,'yh'=2] {'xy','c','zm','yh'}, dimensions={0} | all-to-all | bytes 786432 | tf_op jit(solution)/shard_map/all_to_all | solution.py:362
  59.8 0.0 copy-done.3
  59.8 2.4 %grid_products.1 = bf16[64,40,128]{2,1,0:T(8,128)(2,1)S(1)} custom-call(bf16[64,24,128]{2,1,0:T(8,128)(2,1)S(1)} %all_to_all.20.arrived_ref, bf16[2,512,1024]{2,1,0:T(8,128)(2,1)S(1)} %copy-done.3), custom_call_target="tpu_custom_call" | custom-call | flops 1073741824 | bytes 1048576 | tf_op jit(solution)/shard_map/grid_products/pallas_call | solution.py:363
  62.2 18.0 %all_to_all.21.returned_ref = bf16[64,40,128]{2,1,0:T(8,128)(2,1)S(1)} all-to-all(bf16[64,40,128]{2,1,0:T(8,128)(2,1)S(1)} %grid_products.1), channel_id=1, replica_groups=mesh['xy'=8,'c'=2,'zh'=2,'zl'=4,'zm'=2,'yh'=2] {'xy','c','zm','yh'}, dimensions={0} | all-to-all | bytes 1310720 | tf_op jit(solution)/shard_map/all_to_all | solution.py:372
  80.3 0.0 copy-start.1
  80.3 3.0 %forward_rows.1 = bf16[32,24,128]{2,1,0:T(8,128)(2,1)S(1)} custom-call(f32[2,8,128]{2,1,0:T(8,128)S(1)} %collective-permute-done.settings_ref, bf16[64,40,128]{2,1,0:T(8,128)(2,1)S(1)} %all_to_all.21.returned_ref, bf16[2,1024,512]{2,1,0:T(8,128)(2,1)S(1)} %copy-done.2), custom_call_target="tpu_custom_call" | custom-call | flops 2147483648 | bytes 1048576 | tf_op jit(solution)/shard_map/forward_rows/pallas_call | solution.py:373
  83.2 27.8 %all_to_all.22.parts_ref = bf16[32,24,128]{2,1,0:T(8,128)(2,1)S(1)} all-to-all(bf16[32,24,128]{2,1,0:T(8,128)(2,1)S(1)} %forward_rows.1), channel_id=1, replica_groups=mesh['xy'=8,'c'=2,'zh'=2,'zl'=4,'zm'=2,'yh'=2] {'zl','zm','zh','yh'}, dimensions={0} | all-to-all | bytes 393216 | tf_op jit(solution)/shard_map/all_to_all | solution.py:376
  111.1 0.0 copy-done.1
  111.1 0.9 advance.1
Async XLA Ops:
  1.3 0.9 copy-start
  2.2 35.8 %copy-start.2 = (bf16[2,1024,512]{2,1,0:T(8,128)(2,1)S(1)}, bf16[2,1024,512]{2,1,0:T(8,128)(2,1)}, u32[]{:S(2)}) copy-start(bf16[2,1024,512]{2,1,0:T(8,128)(2,1)} %constant.4.clone.table_ref) | copy-start | bytes 6291460
  3.1 34.9 %all-to-all-start = ((bf16[32,24,128]{2,1,0:T(8,128)(2,1)}), bf16[32,24,128]{2,1,0:T(8,128)(2,1)S(1)}, u32[]{:S(2)}, u32[]{:S(2)}) async-start(bf16[32,24,128]{2,1,0:T(8,128)(2,1)} %get-tuple-element.8), calls=%async_computation | async-start | bytes 393216 | tf_op jit(solution)/shard_map/all_to_all | solution.py:358
  23.1 7.8 %collective-permute-start = (f32[2,8,128]{2,1,0:T(8,128)S(1)}, f32[2,8,128]{2,1,0:T(8,128)S(1)}, u32[]{:S(2)}, u32[]{:S(2)}) collective-permute-start(f32[2,8,128]{2,1,0:T(8,128)S(1)} %bitcast.1), channel_id=1, source_target_pairs={{0,0},{4,64},{8,128},{12,192},{16,256},{20,320},{24,384},{28,448},... | collective-permute-start | bytes 24584 | tf_op jit(solution)/shard_map/ppermute | solution.py:355
  38.0 21.8 %copy-start.3 = (bf16[2,512,1024]{2,1,0:T(8,128)(2,1)S(1)}, bf16[2,512,1024]{2,1,0:T(8,128)(2,1)}, u32[]{:S(2)}) copy-start(bf16[2,512,1024]{2,1,0:T(8,128)(2,1)} %constant.5.clone.table_ref) | copy-start | bytes 6291460
  80.3 30.8 %copy-start.1 = (f32[3,2,32,64]{3,2,1,0:T(8,128)S(1)}, f32[3,2,32,64]{3,2,1,0:T(8,128)}, u32[]{:S(2)}) copy-start(f32[3,2,32,64]{3,2,1,0:T(8,128)} %state_ref.3) | copy-start | bytes 147460

commit v3 on v2

--- a/solution.py
+++ b/solution.py
@@ -134,11 +134,13 @@
     return wave_of(lax.broadcasted_iota(jnp.int32, (rows, LANES), 0) + device * LINES)
 
 
-def spread_kernel(phase_ref, weight_ref, state_ref, out_ref, settings_ref):
+def settings_kernel(phase_ref, weight_ref, settings_ref):
     phase_value = phase_ref[0].astype(F32) * phase_step
     weight = weight_ref[0].astype(F32) * (1.0 / weight_scale)
     settings_ref[...] = jnp.where(lanes_of(8) < 64, phase_value, weight)
 
+
+def spread_kernel(state_ref, out_ref):
     def plane(index):
         return state_ref[index // 2, index % 2]
 
@@ -329,17 +331,14 @@
         out_ref[plane // 2, plane % 2] = result[plane]
 
 
-def call(kernel, name, shape, dtype, scratch, places, flops, outs=None):
+def call(kernel, name, shape, dtype, scratch, places, flops):
     spots = [pl.BlockSpec(memory_space=pltpu.SMEM if p == "s" else pltpu.VMEM) for p in places]
-    whole = pl.BlockSpec(memory_space=pltpu.VMEM)
-    shapes = jax.ShapeDtypeStruct(shape, dtype)
-    extra = jax.ShapeDtypeStruct((8, LANES), F32)
     return pl.pallas_call(
         kernel,
         name=name,
-        out_shape=(shapes, extra) if outs else shapes,
+        out_shape=jax.ShapeDtypeStruct(shape, dtype),
         in_specs=spots,
-        out_specs=(whole, whole) if outs else whole,
+        out_specs=pl.BlockSpec(memory_space=pltpu.VMEM),
         scratch_shapes=[pltpu.VMEM(s, BF16) for s in scratch],
         cost_estimate=pl.CostEstimate(flops=flops, bytes_accessed=1 << 20, transcendentals=0),
         compiler_params=pltpu.CompilerParams(vmem_limit_bytes=VMEM_LIMIT),
@@ -348,9 +347,10 @@
 
 def per_device(spectral_state, phase_index, weight_count):
     tables, turned_tables = fourier_tables()
-    spread, settings = call(
-        spread_kernel, "spread", (32, 24, LANES), BF16, [], "ssv", 1 << 33, True
-    )(phase_index, weight_count, spectral_state)
+    spread = call(spread_kernel, "spread", (32, 24, LANES), BF16, [], "v", 1 << 33)(spectral_state)
+    settings = call(settings_kernel, "settings", (8, LANES), F32, [], "ss", 1 << 12)(
+        phase_index, weight_count
+    )
     settings = lax.all_gather(settings, "c")
     settings = lax.ppermute(
         settings, ("xy", "zh", "zl"), [(8 * i + j, 8 * j + i) for i in range(8) for j in range(8)]

time: 113 us -> 113 us (level)
  blocking collectives: 67.7 us -> 69 us
  waiting for transfers between devices: 10.4 us -> 9.13 us
    all_to_all x1, blocking collectives: 20.1 us -> 21.4 us  [per_device(): arrived = lax.all_to_all(outgoing, GROUP_AXES, 0, 0)]
    all_to_all x1, waiting for transfers between devices: 7.1 us -> 5.96 us  [per_device(): gathered = lax.all_to_all(spread, MAIN_AXES, 0, 0)]
where the time goes in v3:
time: 113 us; the launch traced here: 112 us
  blocking collectives  69 us (61%)
  starting transfers between devices  22.7 us (20%)
  waiting for transfers between devices  9.13 us (8%)
  Pallas kernels  8.9 us (8%)
  between operations  1.35 us (1%)
    all_to_all x1, blocking collectives, per_device(): parts = lax.all_to_all(weighted, MAIN_AXES, 0, 0)  27.8 us
    all_to_all x1, blocking collectives, per_device(): arrived = lax.all_to_all(outgoing, GROUP_AXES, 0, 0)  21.4 us
    all_to_all x1, starting transfers between devices, per_device(): gathered = lax.all_to_all(spread, MAIN_AXES, 0, 0)  18.2 us
    all_to_all x1, blocking collectives, per_device(): returned = lax.all_to_all(outgoing_back, GROUP_AXES, 0, 0)  18 us
    all_to_all x1, waiting for transfers between devices, per_device(): gathered = lax.all_to_all(spread, MAIN_AXES, 0, 0)  5.96 us
    ppermute x1, starting transfers between devices, per_device(): lax.ppermute(settings, ('xy', 'zh', 'zl'), [(8 * i + j, 8 * j + i) for i...  4.44 us
    ppermute x1, waiting for transfers between devices, per_device(): lax.ppermute(settings, ('xy', 'zh', 'zl'), [(8 * i + j, 8 * j + i) for i...  3.18 us
    pallas_call x1, Pallas kernels, per_device(): call(third_kernel, 'forward_rows', (32, 24, LANES), BF16, [(640, N)], 'vv...  2.97 us
  transfers between devices with their start and end apart: 2, of which 2 were waited for; matrix products, arithmetic and copies ran while one was open for 0% of the time, Pallas kernels for 0%

profile of v3, /device:TPU:24, one launch (start us, length us, event | category | flops | bytes accessed | tf_op | source)
XLA Modules:
  0.0 111.9 jit_solution(6168453290427055205)
XLA Ops:
  0.0 0.0 copy-start
  0.0 0.9 copy-done
  0.9 0.0 copy-start.2
  0.9 0.9 spread.1
  1.8 18.2 %all-to-all-start = ((bf16[32,24,128]{2,1,0:T(8,128)(2,1)}), bf16[32,24,128]{2,1,0:T(8,128)(2,1)S(1)}, u32[]{:S(2)}, u32[]{:S(2)}) async-start(bf16[32,24,128]{2,1,0:T(8,128)(2,1)} %spread.1), calls=%async_computation | async-start | bytes 393216 | tf_op jit(solution)/shard_map/all_to_all | solution.py:358
  21.3 1.8 %all-gather = f32[16,128]{1,0:T(8,128)S(1)} all-gather(f32[8,128]{1,0:T(8,128)S(1)} %settings.1), channel_id=2, replica_groups=mesh['xy'=8,'c'=2,'zh'=2,'zl'=4,'zm'=2,'yh'=2] {'c'}, dimensions={0}, use_global_device_ids=true | all-gather | bytes 12288 | tf_op jit(solution)/shard_map/all_gather | solution.py:354
  23.1 4.4 %collective-permute-start = (f32[2,8,128]{2,1,0:T(8,128)S(1)}, f32[2,8,128]{2,1,0:T(8,128)S(1)}, u32[]{:S(2)}, u32[]{:S(2)}) collective-permute-start(f32[2,8,128]{2,1,0:T(8,128)S(1)} %bitcast.1), channel_id=1, source_target_pairs={{0,0},{4,64},{8,128},{12,192},{16,256},{20,320},{24,384},{28,448},... | collective-permute-start | bytes 24584 | tf_op jit(solution)/shard_map/ppermute | solution.py:355
  27.6 3.2 %collective-permute-done.settings_ref = f32[2,8,128]{2,1,0:T(8,128)S(1)} collective-permute-done((f32[2,8,128]{2,1,0:T(8,128)S(1)}, f32[2,8,128]{2,1,0:T(8,128)S(1)}, u32[]{:S(2)}, u32[]{:S(2)}) %collective-permute-start) | collective-permute-done | bytes 8224 | tf_op jit(solution)/shard_map/ppermute | solution.py:355
  30.8 6.0 %all-to-all-done.gathered_ref = bf16[32,24,128]{2,1,0:T(8,128)(2,1)S(1)} async-done(((bf16[32,24,128]{2,1,0:T(8,128)(2,1)}), bf16[32,24,128]{2,1,0:T(8,128)(2,1)S(1)}, u32[]{:S(2)}, u32[]{:S(2)}) %all-to-all-start) | async-done | bytes 196640 | tf_op jit(solution)/shard_map/all_to_all | solution.py:358
  36.7 0.0 copy-done.2
  36.7 0.0 copy-start.3
  36.7 1.8 %inverse_rows.1 = bf16[64,24,128]{2,1,0:T(8,128)(2,1)S(1)} custom-call(f32[2,8,128]{2,1,0:T(8,128)S(1)} %collective-permute-done.settings_ref, bf16[32,24,128]{2,1,0:T(8,128)(2,1)S(1)} %all-to-all-done.gathered_ref, bf16[2,1024,512]{2,1,0:T(8,128)(2,1)S(1)} %copy-done.2), custom_call_target="tpu_custom_call" | custom-call | flops 1073741824 | bytes 1048576 | tf_op jit(solution)/shard_map/inverse_rows/pallas_call | solution.py:359
  38.5 21.4 %all_to_all.20.arrived_ref = bf16[64,24,128]{2,1,0:T(8,128)(2,1)S(1)} all-to-all(bf16[64,24,128]{2,1,0:T(8,128)(2,1)S(1)} %inverse_rows.1), channel_id=1, replica_groups=mesh['xy'=8,'c'=2,'zh'=2,'zl'=4,'zm'=2,'yh'=2] {'xy','c','zm','yh'}, dimensions={0} | all-to-all | bytes 786432 | tf_op jit(solution)/shard_map/all_to_all | solution.py:362
  59.8 0.0 copy-done.3
  59.9 2.4 %grid_products.1 = bf16[64,40,128]{2,1,0:T(8,128)(2,1)S(1)} custom-call(bf16[64,24,128]{2,1,0:T(8,128)(2,1)S(1)} %all_to_all.20.arrived_ref, bf16[2,512,1024]{2,1,0:T(8,128)(2,1)S(1)} %copy-done.3), custom_call_target="tpu_custom_call" | custom-call | flops 1073741824 | bytes 1048576 | tf_op jit(solution)/shard_map/grid_products/pallas_call | solution.py:363
  62.2 18.0 %all_to_all.21.returned_ref = bf16[64,40,128]{2,1,0:T(8,128)(2,1)S(1)} all-to-all(bf16[64,40,128]{2,1,0:T(8,128)(2,1)S(1)} %grid_products.1), channel_id=1, replica_groups=mesh['xy'=8,'c'=2,'zh'=2,'zl'=4,'zm'=2,'yh'=2] {'xy','c','zm','yh'}, dimensions={0} | all-to-all | bytes 1310720 | tf_op jit(solution)/shard_map/all_to_all | solution.py:372
  80.3 0.0 copy-start.1
  80.3 3.0 %forward_rows.1 = bf16[32,24,128]{2,1,0:T(8,128)(2,1)S(1)} custom-call(f32[2,8,128]{2,1,0:T(8,128)S(1)} %collective-permute-done.settings_ref, bf16[64,40,128]{2,1,0:T(8,128)(2,1)S(1)} %all_to_all.21.returned_ref, bf16[2,1024,512]{2,1,0:T(8,128)(2,1)S(1)} %copy-done.2), custom_call_target="tpu_custom_call" | custom-call | flops 2147483648 | bytes 1048576 | tf_op jit(solution)/shard_map/forward_rows/pallas_call | solution.py:373
  83.3 27.8 %all_to_all.22.parts_ref = bf16[32,24,128]{2,1,0:T(8,128)(2,1)S(1)} all-to-all(bf16[32,24,128]{2,1,0:T(8,128)(2,1)S(1)} %forward_rows.1), channel_id=1, replica_groups=mesh['xy'=8,'c'=2,'zh'=2,'zl'=4,'zm'=2,'yh'=2] {'zl','zm','zh','yh'}, dimensions={0} | all-to-all | bytes 393216 | tf_op jit(solution)/shard_map/all_to_all | solution.py:376
  111.1 0.0 copy-done.1
  111.1 0.9 advance.1
  (1 shorter events, 0.0 us)
Async XLA Ops:
  0.0 0.9 copy-start
  0.9 35.8 %copy-start.2 = (bf16[2,1024,512]{2,1,0:T(8,128)(2,1)S(1)}, bf16[2,1024,512]{2,1,0:T(8,128)(2,1)}, u32[]{:S(2)}) copy-start(bf16[2,1024,512]{2,1,0:T(8,128)(2,1)} %constant.4.clone.table_ref) | copy-start | bytes 6291460
  1.8 34.9 %all-to-all-start = ((bf16[32,24,128]{2,1,0:T(8,128)(2,1)}), bf16[32,24,128]{2,1,0:T(8,128)(2,1)S(1)}, u32[]{:S(2)}, u32[]{:S(2)}) async-start(bf16[32,24,128]{2,1,0:T(8,128)(2,1)} %spread.1), calls=%async_computation | async-start | bytes 393216 | tf_op jit(solution)/shard_map/all_to_all | solution.py:358
  23.1 7.6 %collective-permute-start = (f32[2,8,128]{2,1,0:T(8,128)S(1)}, f32[2,8,128]{2,1,0:T(8,128)S(1)}, u32[]{:S(2)}, u32[]{:S(2)}) collective-permute-start(f32[2,8,128]{2,1,0:T(8,128)S(1)} %bitcast.1), channel_id=1, source_target_pairs={{0,0},{4,64},{8,128},{12,192},{16,256},{20,320},{24,384},{28,448},... | collective-permute-start | bytes 24584 | tf_op jit(solution)/shard_map/ppermute | solution.py:355
  36.7 23.1 %copy-start.3 = (bf16[2,512,1024]{2,1,0:T(8,128)(2,1)S(1)}, bf16[2,512,1024]{2,1,0:T(8,128)(2,1)}, u32[]{:S(2)}) copy-start(bf16[2,512,1024]{2,1,0:T(8,128)(2,1)} %constant.5.clone.table_ref) | copy-start | bytes 6291460
  80.3 30.8 %copy-start.1 = (f32[3,2,32,64]{3,2,1,0:T(8,128)S(1)}, f32[3,2,32,64]{3,2,1,0:T(8,128)}, u32[]{:S(2)}) copy-start(f32[3,2,32,64]{3,2,1,0:T(8,128)} %state_ref.3) | copy-start | bytes 147460

commit v4 on v3

--- a/solution.py
+++ b/solution.py
@@ -157,7 +157,7 @@
             out_ref[slot(4 * block + part)] = message
 
 
-def first_kernel(settings_ref, gathered_ref, table_ref, out_ref, rotated):
+def first_kernel(settings_ref, gathered_ref, table_ref, out_ref, terms_ref, rotated):
     wave_columns = own_columns(LINES)
     for group in range(8):
         lanes = slice(LANES * group, LANES * (group + 1))
@@ -170,6 +170,7 @@
         for phase in range(2):
             phase_value = settings_ref[phase, :1, :1]
             terms = exponential_terms(wave_rows, wave_columns, phase_value)
+            terms_ref[2 * phase, :, lanes], terms_ref[2 * phase + 1, :, lanes] = terms
             result = wave_exponential(planes, wave_rows, wave_columns, *terms)
             for plane in range(6):
                 start = 96 * phase + LINES * plane
@@ -252,7 +253,7 @@
 PRODUCT_ORDER = ((0, 0), (0, 2), (0, 3), (1, 0), (1, 2), (1, 3), (0, 1), (0, 4))
 
 
-def third_kernel(settings_ref, returned_ref, table_ref, out_ref, lines):
+def third_kernel(settings_ref, terms_ref, returned_ref, table_ref, out_ref, lines):
     wave_columns = own_columns(LINES)
     for group in range(8):
         lanes = slice(LANES * group, LANES * (group + 1))
@@ -279,7 +280,6 @@
             wave_rows = wave_of(lanes_of(LINES) + LANES * group)
             total = None
             for phase in range(2):
-                phase_value = settings_ref[phase, :1, :1]
                 weight = settings_ref[phase, :1, 64:65]
                 real, imag = [], []
                 for product in range(5):
@@ -294,7 +294,9 @@
                     tendency.append(
                         -(wave_rows * real[toward_east] + wave_columns * real[toward_north])
                     )
-                sine_term, cosine_term = exponential_terms(wave_rows, wave_columns, phase_value)
+                own = slice(LANES * group, LANES * (group + 1))
+                sine_term = terms_ref[2 * phase, :, own]
+                cosine_term = terms_ref[2 * phase + 1, :, own]
                 result = wave_exponential(
                     tendency, wave_rows, wave_columns, -sine_term, cosine_term
                 )
@@ -331,14 +333,16 @@
         out_ref[plane // 2, plane % 2] = result[plane]
 
 
-def call(kernel, name, shape, dtype, scratch, places, flops):
+def call(kernel, name, shape, dtype, scratch, places, flops, extra=None):
     spots = [pl.BlockSpec(memory_space=pltpu.SMEM if p == "s" else pltpu.VMEM) for p in places]
+    whole = pl.BlockSpec(memory_space=pltpu.VMEM)
+    shapes = jax.ShapeDtypeStruct(shape, dtype)
     return pl.pallas_call(
         kernel,
         name=name,
-        out_shape=jax.ShapeDtypeStruct(shape, dtype),
+        out_shape=(shapes, jax.ShapeDtypeStruct(extra, F32)) if extra else shapes,
         in_specs=spots,
-        out_specs=pl.BlockSpec(memory_space=pltpu.VMEM),
+        out_specs=(whole, whole) if extra else whole,
         scratch_shapes=[pltpu.VMEM(s, BF16) for s in scratch],
         cost_estimate=pl.CostEstimate(flops=flops, bytes_accessed=1 << 20, transcendentals=0),
         compiler_params=pltpu.CompilerParams(vmem_limit_bytes=VMEM_LIMIT),
@@ -356,7 +360,7 @@
         settings, ("xy", "zh", "zl"), [(8 * i + j, 8 * j + i) for i in range(8) for j in range(8)]
     )
     gathered = lax.all_to_all(spread, MAIN_AXES, 0, 0)
-    outgoing = call(first_kernel, "inverse_rows", (64, 24, LANES), BF16, [(384, N)], "vvv", 1 << 30)(
+    outgoing, terms = call(first_kernel, "inverse_rows", (64, 24, LANES), BF16, [(384, N)], "vvv", 1 << 30, (4, LINES, N))(
         settings, gathered, tables
     )
     arrived = lax.all_to_all(outgoing, GROUP_AXES, 0, 0)
@@ -370,8 +374,8 @@
         1 << 30,
     )(arrived, turned_tables)
     returned = lax.all_to_all(outgoing_back, GROUP_AXES, 0, 0)
-    weighted = call(third_kernel, "forward_rows", (32, 24, LANES), BF16, [(640, N)], "vvv", 1 << 31)(
-        settings, returned, tables
+    weighted = call(third_kernel, "forward_rows", (32, 24, LANES), BF16, [(640, N)], "vvvv", 1 << 31)(
+        settings, terms, returned, tables
     )
     parts = lax.all_to_all(weighted, MAIN_AXES, 0, 0)
     return call(last_kernel, "advance", spectral_state.shape, F32, [], "vv", 1 << 24)(spectral_state, parts)

time: 113 us -> 113 us (level)
  no operation moved by 1% of the time
where the time goes in v4:
time: 113 us; the launch traced here: 112 us
  blocking collectives  69 us (61%)
  starting transfers between devices  22.7 us (20%)
  waiting for transfers between devices  9.13 us (8%)
  Pallas kernels  8.74 us (8%)
  between operations  1.35 us (1%)
    all_to_all x1, blocking collectives, per_device(): parts = lax.all_to_all(weighted, MAIN_AXES, 0, 0)  27.8 us
    all_to_all x1, blocking collectives, per_device(): arrived = lax.all_to_all(outgoing, GROUP_AXES, 0, 0)  21.4 us
    all_to_all x1, starting transfers between devices, per_device(): gathered = lax.all_to_all(spread, MAIN_AXES, 0, 0)  18.2 us
    all_to_all x1, blocking collectives, per_device(): returned = lax.all_to_all(outgoing_back, GROUP_AXES, 0, 0)  18 us
    all_to_all x1, waiting for transfers between devices, per_device(): gathered = lax.all_to_all(spread, MAIN_AXES, 0, 0)  5.96 us
    ppermute x1, starting transfers between devices, per_device(): lax.ppermute(settings, ('xy', 'zh', 'zl'), [(8 * i + j, 8 * j + i) for i...  4.44 us
    ppermute x1, waiting for transfers between devices, per_device(): lax.ppermute(settings, ('xy', 'zh', 'zl'), [(8 * i + j, 8 * j + i) for i...  3.18 us
    pallas_call x1, Pallas kernels, per_device(): call(third_kernel, 'forward_rows', (32, 24, LANES), BF16, [(640, N)], 'vv...  2.8 us
  transfers between devices with their start and end apart: 2, of which 2 were waited for; matrix products, arithmetic and copies ran while one was open for 0% of the time, Pallas kernels for 0%

profile of v4, /device:TPU:24, one launch (start us, length us, event | category | flops | bytes accessed | tf_op | source)
XLA Modules:
  0.0 111.8 jit_solution(16803421811315315872)
XLA Ops:
  0.0 0.0 copy-start
  0.0 0.9 copy-done
  0.9 0.0 copy-start.2
  0.9 0.9 spread.1
  1.8 18.2 %all-to-all-start = ((bf16[32,24,128]{2,1,0:T(8,128)(2,1)}), bf16[32,24,128]{2,1,0:T(8,128)(2,1)S(1)}, u32[]{:S(2)}, u32[]{:S(2)}) async-start(bf16[32,24,128]{2,1,0:T(8,128)(2,1)} %spread.1), calls=%async_computation | async-start | bytes 393216 | tf_op jit(solution)/shard_map/all_to_all | solution.py:362
  21.3 1.8 %all-gather = f32[16,128]{1,0:T(8,128)S(1)} all-gather(f32[8,128]{1,0:T(8,128)S(1)} %settings.1), channel_id=2, replica_groups=mesh['xy'=8,'c'=2,'zh'=2,'zl'=4,'zm'=2,'yh'=2] {'c'}, dimensions={0}, use_global_device_ids=true | all-gather | bytes 12288 | tf_op jit(solution)/shard_map/all_gather | solution.py:358
  23.1 4.4 %collective-permute-start = (f32[2,8,128]{2,1,0:T(8,128)S(1)}, f32[2,8,128]{2,1,0:T(8,128)S(1)}, u32[]{:S(2)}, u32[]{:S(2)}) collective-permute-start(f32[2,8,128]{2,1,0:T(8,128)S(1)} %bitcast.1), channel_id=1, source_target_pairs={{0,0},{4,64},{8,128},{12,192},{16,256},{20,320},{24,384},{28,448},... | collective-permute-start | bytes 24584 | tf_op jit(solution)/shard_map/ppermute | solution.py:359
  27.6 3.2 %collective-permute-done.settings_ref = f32[2,8,128]{2,1,0:T(8,128)S(1)} collective-permute-done((f32[2,8,128]{2,1,0:T(8,128)S(1)}, f32[2,8,128]{2,1,0:T(8,128)S(1)}, u32[]{:S(2)}, u32[]{:S(2)}) %collective-permute-start) | collective-permute-done | bytes 8224 | tf_op jit(solution)/shard_map/ppermute | solution.py:359
  30.8 6.0 %all-to-all-done.gathered_ref = bf16[32,24,128]{2,1,0:T(8,128)(2,1)S(1)} async-done(((bf16[32,24,128]{2,1,0:T(8,128)(2,1)}), bf16[32,24,128]{2,1,0:T(8,128)(2,1)S(1)}, u32[]{:S(2)}, u32[]{:S(2)}) %all-to-all-start) | async-done | bytes 196640 | tf_op jit(solution)/shard_map/all_to_all | solution.py:362
  36.7 0.0 copy-done.2
  36.7 0.0 copy-start.3
  36.7 1.8 %inverse_rows.1 = (bf16[64,24,128]{2,1,0:T(8,128)(2,1)S(1)}, f32[4,16,1024]{2,1,0:T(8,128)S(1)}) custom-call(f32[2,8,128]{2,1,0:T(8,128)S(1)} %collective-permute-done.settings_ref, bf16[32,24,128]{2,1,0:T(8,128)(2,1)S(1)} %all-to-all-done.gathered_ref, bf16[2,1024,512]{2,1,0:T(8,128)(2,1)S(1)} %copy-done.2), custom_call_target="tpu_custom_call" | custom-call | flops 1073741824 | bytes 1048576 | tf_op jit(solution)/shard_map/inverse_rows/pallas_call | solution.py:363
  38.5 21.4 %all_to_all.20.arrived_ref = bf16[64,24,128]{2,1,0:T(8,128)(2,1)S(1)} all-to-all(bf16[64,24,128]{2,1,0:T(8,128)(2,1)S(1)} %get-tuple-element.8), channel_id=1, replica_groups=mesh['xy'=8,'c'=2,'zh'=2,'zl'=4,'zm'=2,'yh'=2] {'xy','c','zm','yh'}, dimensions={0} | all-to-all | bytes 786432 | tf_op jit(solution)/shard_map/all_to_all | solution.py:366
  59.9 0.0 copy-done.3
  59.9 2.4 %grid_products.1 = bf16[64,40,128]{2,1,0:T(8,128)(2,1)S(1)} custom-call(bf16[64,24,128]{2,1,0:T(8,128)(2,1)S(1)} %all_to_all.20.arrived_ref, bf16[2,512,1024]{2,1,0:T(8,128)(2,1)S(1)} %copy-done.3), custom_call_target="tpu_custom_call" | custom-call | flops 1073741824 | bytes 1048576 | tf_op jit(solution)/shard_map/grid_products/pallas_call | solution.py:367
  62.3 18.0 %all_to_all.21.returned_ref = bf16[64,40,128]{2,1,0:T(8,128)(2,1)S(1)} all-to-all(bf16[64,40,128]{2,1,0:T(8,128)(2,1)S(1)} %grid_products.1), channel_id=1, replica_groups=mesh['xy'=8,'c'=2,'zh'=2,'zl'=4,'zm'=2,'yh'=2] {'xy','c','zm','yh'}, dimensions={0} | all-to-all | bytes 1310720 | tf_op jit(solution)/shard_map/all_to_all | solution.py:376
  80.3 0.0 copy-start.1
  80.3 2.8 %forward_rows.1 = bf16[32,24,128]{2,1,0:T(8,128)(2,1)S(1)} custom-call(f32[2,8,128]{2,1,0:T(8,128)S(1)} %collective-permute-done.settings_ref, f32[4,16,1024]{2,1,0:T(8,128)S(1)} %get-tuple-element.7.terms_ref, bf16[64,40,128]{2,1,0:T(8,128)(2,1)S(1)} %all_to_all.21.returned_ref, bf16[2,1024,512]{2,1,0:T(8,128)(2,1)S(1)} %copy-done.2), custom_call_target="tpu_custom_call" | custom-call | flops 2147483648 | bytes 1048576 | tf_op jit(solution)/shard_map/forward_rows/pallas_call | solution.py:377
  83.1 27.8 %all_to_all.22.parts_ref = bf16[32,24,128]{2,1,0:T(8,128)(2,1)S(1)} all-to-all(bf16[32,24,128]{2,1,0:T(8,128)(2,1)S(1)} %forward_rows.1), channel_id=1, replica_groups=mesh['xy'=8,'c'=2,'zh'=2,'zl'=4,'zm'=2,'yh'=2] {'zl','zm','zh','yh'}, dimensions={0} | all-to-all | bytes 393216 | tf_op jit(solution)/shard_map/all_to_all | solution.py:380
  110.9 0.0 copy-done.1
  110.9 0.9 advance.1
  (1 shorter events, 0.0 us)
Async XLA Ops:
  0.0 0.9 copy-start
  0.9 35.8 %copy-start.2 = (bf16[2,1024,512]{2,1,0:T(8,128)(2,1)S(1)}, bf16[2,1024,512]{2,1,0:T(8,128)(2,1)}, u32[]{:S(2)}) copy-start(bf16[2,1024,512]{2,1,0:T(8,128)(2,1)} %constant.4.clone.table_ref) | copy-start | bytes 6291460
  1.8 34.9 %all-to-all-start = ((bf16[32,24,128]{2,1,0:T(8,128)(2,1)}), bf16[32,24,128]{2,1,0:T(8,128)(2,1)S(1)}, u32[]{:S(2)}, u32[]{:S(2)}) async-start(bf16[32,24,128]{2,1,0:T(8,128)(2,1)} %spread.1), calls=%async_computation | async-start | bytes 393216 | tf_op jit(solution)/shard_map/all_to_all | solution.py:362
  23.1 7.6 %collective-permute-start = (f32[2,8,128]{2,1,0:T(8,128)S(1)}, f32[2,8,128]{2,1,0:T(8,128)S(1)}, u32[]{:S(2)}, u32[]{:S(2)}) collective-permute-start(f32[2,8,128]{2,1,0:T(8,128)S(1)} %bitcast.1), channel_id=1, source_target_pairs={{0,0},{4,64},{8,128},{12,192},{16,256},{20,320},{24,384},{28,448},... | collective-permute-start | bytes 24584 | tf_op jit(solution)/shard_map/ppermute | solution.py:359
  36.7 23.1 %copy-start.3 = (bf16[2,512,1024]{2,1,0:T(8,128)(2,1)S(1)}, bf16[2,512,1024]{2,1,0:T(8,128)(2,1)}, u32[]{:S(2)}) copy-start(bf16[2,512,1024]{2,1,0:T(8,128)(2,1)} %constant.5.clone.table_ref) | copy-start | bytes 6291460
  80.3 30.6 %copy-start.1 = (f32[3,2,32,64]{3,2,1,0:T(8,128)S(1)}, f32[3,2,32,64]{3,2,1,0:T(8,128)}, u32[]{:S(2)}) copy-start(f32[3,2,32,64]{3,2,1,0:T(8,128)} %state_ref.3) | copy-start | bytes 147460
